TPU v7x, 256 devices: a whole 4x4x8 slice. The times are simulated.
256 devices in a mesh: wave: 16 (over z, core), col: 16 (over x, y).
Axes of the slice: x: 4, y: 4, z: 8, core: 2. Of those that a mesh axis runs over, the one named last changes fastest.
Arguments:
- divergence: float32 [256, 2, 128, 1024], P('wave', None, 'col'), may hold values from -6 to 6
- analysis: float32 [128, 128], replicated, may hold values from -0.5 to 0.5
- synthesis: float32 [128, 128], replicated, may hold values from -0.5 to 0.5
- helmholtz: float32 [128], replicated, may hold values from 3e-07 to 0.0003
- legendre: bfloat16 [256, 1024, 1024], P('wave', None, 'col'), may hold values from -0.1875 to 0.1875
- wavenumbers: int32 [256], replicated, may hold values from 0 to 1023, as said below
- cycle_points: int32 [1024], replicated, may hold values from 2048 to 4096, as said below
Outputs:
- grid_field: bfloat16 [16, 64, 4096, 128], P('col', 'wave')
Inputs may be any that keep to these rules, and one draw needn't show every extreme that they name: Distinct values; slots 2 i and 2 i + 1 hold two wavenumbers that add up to 1023. `cycle_points`: multiples of 16.
All inputs are finite; a program needn't handle non-finite values.
Results may differ from a plain program's by a relative error of at most 0.0062.
Values may be sent and summed in bfloat16 or wider, within the bound.
A program may use at most 64 MiB of HBM per device.

v0:
```python
import math

import jax
import jax.numpy as jnp
from jax import lax
from jax.sharding import PartitionSpec as P

LON = 4096


def cycle_basis(wavenumbers, point_count, length, window):
    span = 64
    coarse_index = jnp.arange(length // span, dtype=jnp.int32) * span
    fine_index = jnp.arange(span, dtype=jnp.int32)
    scale = 2.0 * math.pi / point_count.astype(jnp.float32)
    coarse_angle = (coarse_index[:, None] * wavenumbers[None, :] % point_count).astype(
        jnp.float32
    ) * scale
    fine_angle = (fine_index[:, None] * wavenumbers[None, :] % point_count).astype(
        jnp.float32
    ) * scale
    coarse_cos, coarse_sin = (jnp.cos(coarse_angle), jnp.sin(coarse_angle))
    fine_cos, fine_sin = (jnp.cos(fine_angle), jnp.sin(fine_angle))
    cosine = (
        coarse_cos[:, None, :] * fine_cos[None, :, :]
        - coarse_sin[:, None, :] * fine_sin[None, :, :]
    )
    sine = (
        coarse_sin[:, None, :] * fine_cos[None, :, :]
        + coarse_cos[:, None, :] * fine_sin[None, :, :]
    )
    cosine = cosine.reshape(length, wavenumbers.shape[0])
    sine = sine.reshape(length, wavenumbers.shape[0])
    column = jnp.arange(length, dtype=jnp.int32)
    weight = jnp.where(wavenumbers == 0, 1.0, 2.0).astype(jnp.float32) / math.sqrt(window)
    valid = column[:, None] < point_count
    cosine = jnp.where(valid, weight[None, :] * cosine, 0.0)
    sine = jnp.where(valid, -weight[None, :] * sine, 0.0)
    return (
        jnp.stack([cosine, sine], axis=2)
        .reshape(length, 2 * wavenumbers.shape[0])
        .astype(jnp.bfloat16)
    )


def on_device(divergence, analysis, synthesis, helmholtz, legendre, wavenumbers, cycle_points):
    slot_count = divergence.shape[0]
    level_count = analysis.shape[0]
    lat_local = legendre.shape[2]
    wave_count = lax.axis_size("wave")
    wave_index = lax.axis_index("wave")
    col_index = lax.axis_index("col")
    own_waves = lax.dynamic_slice_in_dim(wavenumbers, wave_index * slot_count, slot_count)
    whole = lax.all_gather(divergence, "col", axis=2, tiled=True)
    degree_index = jnp.arange(whole.shape[3], dtype=jnp.int32)
    degree = degree_index.astype(jnp.float32)
    factor = 1.0 / (1.0 + helmholtz[:, None] * (degree * (degree + 1.0))[None, :])
    modes = jnp.einsum("kl,srln->srkn", analysis, whole, precision=lax.Precision.HIGHEST)
    solved = jnp.einsum(
        "lk,srkn->srln", synthesis, modes * factor[None, None], precision=lax.Precision.HIGHEST
    )
    keep = degree_index[None, :] >= own_waves[:, None]
    coefs = jnp.where(keep[:, None, None, :], solved, 0.0).astype(jnp.bfloat16)
    summed_field = jnp.einsum("srln,snt->strl", coefs, legendre, preferred_element_type=jnp.float32)
    field = summed_field.astype(jnp.bfloat16)
    bands = lax.all_to_all(field, "wave", split_axis=1, concat_axis=0, tiled=True)
    band_size = lat_local // wave_count
    window = slot_count * wave_count

    def synthesize(offset):
        latitude = col_index * lat_local + wave_index * band_size + offset
        point_count = lax.dynamic_index_in_dim(cycle_points, latitude, 0, keepdims=False)
        basis = cycle_basis(wavenumbers, point_count, LON, window)
        values = lax.dynamic_index_in_dim(bands, offset, 1, keepdims=False).reshape(
            2 * window, level_count
        )
        return jnp.dot(basis, values, preferred_element_type=jnp.float32).astype(jnp.bfloat16)

    grid = lax.map(synthesize, jnp.arange(band_size, dtype=jnp.int32))
    return grid[None]


def solution(mesh):
    placed = (P("wave", None, "col", None), P(), P(), P(), P("wave", None, "col"), P(), P())
    return jax.shard_map(
        on_device,
        mesh=mesh,
        in_specs=placed,
        out_specs=P("col", "wave", None, None),
        check_vma=False,
    )
```

profile of v0, /device:TPU:1, one launch (start us, length us, event | category | flops | bytes accessed | tf_op | source)
XLA Modules:
  0.0 358.5 jit_solution(7530252517866172301)
XLA Ops:
  6.5 0.0 copy-start
  6.5 0.0 all-gather.2.cloned.1.call-start
  6.5 0.7 all-gather.2.cloned.1.call-update
  7.3 0.8 dynamic_slice.21
  8.0 0.1 iota_compare_fusion.1
  8.1 0.9 add_divide_fusion
  9.0 0.0 copy-start.3
  9.0 121.0 %all-gather.2.cloned.1.call-done = f32[16,2,128,1024]{3,2,1,0:T(8,128)} async-done(((f32[16,2,8,1024]{3,2,1,0:T(8,128)}), f32[16,2,128,1024]{3,2,1,0:T(8,128)}) %all-gather.2.cloned.1.call-update) | async-done | bytes 16777232 | tf_op jit(solution)/shard_map/all_gather | solution.py:54
  130.0 29.2 %fusion.40 = f32[16,2,1024,128]{3,2,1,0:T(8,128)S(1)} fusion(f32[16,2,128,1024]{3,2,1,0:T(8,128)} %all-gather.2.cloned.1.call-done, f32[128,128]{1,0:T(8,128)} %param.10), kind=kOutput, calls=%fused_computation.49 | convolution fusion | flops 6442450944 | bytes 33619968 | tf_op jit(solution)/shard_map/kl,srln->srkn/dot_general | solution.py:58
  159.2 0.0 copy-done.3
  159.2 14.1 %select_convert_fusion = bf16[16,2,1024,128]{3,2,1,0:T(8,128)(2,1)S(1)} fusion(f32[16,2,1024,128]{3,2,1,0:T(8,128)S(1)} %fusion.40, f32[128,1024]{0,1:T(8,128)S(1)} %add_divide_fusion, pred[16,1024]{1,0:T(8,128)(4,1)S(1)} %iota_compare_fusion.1, f32[128,128]{1,0:T(8,128)S(1)} %copy-done.3), kind=kOutput, calls=%fused_computation.40 | convolution fusion | flops 6455033856 | bytes 25772032 | tf_op jit(solution)/shard_map/lk,srkn->srln/dot_general | solution.py:59
  173.3 0.0 copy-done
  173.3 0.0 copy-start.2
  173.3 1.6 fusion.34
  174.9 1.3 copy.13
  176.2 7.7 %all-to-all-start = ((bf16[16,64,2,128]{3,2,0,1:T(2,128)(2,1)}), bf16[16,64,2,128]{3,2,0,1:T(2,128)(2,1)S(1)}, u32[]{:S(2)}, u32[]{:S(2)}) async-start(bf16[16,64,2,128]{3,2,0,1:T(2,128)(2,1)} %copy.13), calls=%async_computation | async-start | bytes 1048576 | tf_op jit(solution)/shard_map/all_to_all | solution.py:66
  183.9 17.3 %all-to-all-done = bf16[16,64,2,128]{3,2,0,1:T(2,128)(2,1)S(1)} async-done(((bf16[16,64,2,128]{3,2,0,1:T(2,128)(2,1)}), bf16[16,64,2,128]{3,2,0,1:T(2,128)(2,1)S(1)}, u32[]{:S(2)}, u32[]{:S(2)}) %all-to-all-start) | async-done | bytes 524320 | tf_op jit(solution)/shard_map/all_to_all | solution.py:66
  201.2 0.4 copy.14
  201.7 148.4 %while.12 = (s32[]{:T(128)}, bf16[4,4096,128]{2,1,0:T(8,128)(2,1)}, s32[4]{0:T(128)S(1)}, s32[]{:T(128)}, s32[1024]{0:T(1024)}, /*index=5*/s32[256]{0:T(256)S(1)...) while((s32[]{:T(128)}, bf16[4,4096,128]{2,1,0:T(8,128)(2,1)}, ...), condition=%wide.region_1.2_spmd, body=%wide.region_0.1_spmd.sunk | while | flops 552408128 | bytes 52312872 | solution.py:79
  201.7 0.6 dynamic_slice.27
  204.5 1.3 dynamic_slice.28
  207.5 0.6 iota_compare_fusion.3
  208.1 0.1 constant_dynamic-slice_fusion.2
  208.2 1.8 fusion.53
  210.0 1.2 multiply_subtract_fusion.2
  211.3 2.2 fusion.55
  213.4 2.3 pad_maximum_fusion.2
  215.8 11.3 %copy.20 = bf16[4096,256,2]{0,2,1:T(2,128)(2,1)} copy(bf16[4096,256,2]{1,0,2:T(8,128)(2,1)} %pad_maximum_fusion.2) | data formatting | bytes 8388608 | tf_op jit(solution)/shard_map/while/body/eval_jaxpr/stack | solution.py:40
  227.1 7.3 %convert_element_type.105 = bf16[4096,512]{0,1:T(8,128)(2,1)} reshape(bf16[4096,256,2]{0,2,1:T(2,128)(2,1)} %copy.20) | data formatting | bytes 8388608 | tf_op jit(solution)/shard_map/while/body/eval_jaxpr/convert_element_type | solution.py:42
  234.3 4.5 %fusion.56 = bf16[4,4096,128]{2,1,0:T(8,128)(2,1)} fusion(bf16[4,4096,128]{2,1,0:T(8,128)(2,1)} %get-tuple-element.199, s32[]{:T(128)S(6)} %copy.24, bf16[4096,512]{0,1:T(8,128)(2,1)} %convert_element_type.105, bf16[512,128]{1,0:T(8,128)(2,1)S(1)} %bitcast.76), kind=kOutput, calls=%fused_computation.2.clone.1 | convolution fusion | flops 537395200 | bytes 5373956 | tf_op jit(solution)/shard_map/while/body/eval_jaxpr/dot_general | solution.py:77
  238.8 0.6 dynamic_slice.27
  241.6 1.3 dynamic_slice.28
  244.7 0.6 iota_compare_fusion.3
  245.2 0.1 constant_dynamic-slice_fusion.2
  245.3 1.8 fusion.53
  247.1 1.2 multiply_subtract_fusion.2
  248.4 2.2 fusion.55
  250.5 2.3 pad_maximum_fusion.2
  252.9 11.3 %copy.20 = bf16[4096,256,2]{0,2,1:T(2,128)(2,1)} copy(bf16[4096,256,2]{1,0,2:T(8,128)(2,1)} %pad_maximum_fusion.2) | data formatting | bytes 8388608 | tf_op jit(solution)/shard_map/while/body/eval_jaxpr/stack | solution.py:40
  264.2 7.3 %convert_element_type.105 = bf16[4096,512]{0,1:T(8,128)(2,1)} reshape(bf16[4096,256,2]{0,2,1:T(2,128)(2,1)} %copy.20) | data formatting | bytes 8388608 | tf_op jit(solution)/shard_map/while/body/eval_jaxpr/convert_element_type | solution.py:42
  271.4 4.5 %fusion.56 = bf16[4,4096,128]{2,1,0:T(8,128)(2,1)} fusion(bf16[4,4096,128]{2,1,0:T(8,128)(2,1)} %get-tuple-element.199, s32[]{:T(128)S(6)} %copy.24, bf16[4096,512]{0,1:T(8,128)(2,1)} %convert_element_type.105, bf16[512,128]{1,0:T(8,128)(2,1)S(1)} %bitcast.76), kind=kOutput, calls=%fused_computation.2.clone.1 | convolution fusion | flops 537395200 | bytes 5373956 | tf_op jit(solution)/shard_map/while/body/eval_jaxpr/dot_general | solution.py:77
  275.9 0.6 dynamic_slice.27
  278.7 1.3 dynamic_slice.28
  281.8 0.6 iota_compare_fusion.3
  282.3 0.1 constant_dynamic-slice_fusion.2
  282.4 1.8 fusion.53
  284.3 1.2 multiply_subtract_fusion.2
  285.5 2.2 fusion.55
  287.6 2.3 pad_maximum_fusion.2
  290.0 11.3 %copy.20 = bf16[4096,256,2]{0,2,1:T(2,128)(2,1)} copy(bf16[4096,256,2]{1,0,2:T(8,128)(2,1)} %pad_maximum_fusion.2) | data formatting | bytes 8388608 | tf_op jit(solution)/shard_map/while/body/eval_jaxpr/stack | solution.py:40
  301.3 7.3 %convert_element_type.105 = bf16[4096,512]{0,1:T(8,128)(2,1)} reshape(bf16[4096,256,2]{0,2,1:T(2,128)(2,1)} %copy.20) | data formatting | bytes 8388608 | tf_op jit(solution)/shard_map/while/body/eval_jaxpr/convert_element_type | solution.py:42
  308.5 4.5 %fusion.56 = bf16[4,4096,128]{2,1,0:T(8,128)(2,1)} fusion(bf16[4,4096,128]{2,1,0:T(8,128)(2,1)} %get-tuple-element.199, s32[]{:T(128)S(6)} %copy.24, bf16[4096,512]{0,1:T(8,128)(2,1)} %convert_element_type.105, bf16[512,128]{1,0:T(8,128)(2,1)S(1)} %bitcast.76), kind=kOutput, calls=%fused_computation.2.clone.1 | convolution fusion | flops 537395200 | bytes 5373956 | tf_op jit(solution)/shard_map/while/body/eval_jaxpr/dot_general | solution.py:77
  313.0 0.6 dynamic_slice.27
  315.8 1.3 dynamic_slice.28
  318.9 0.6 iota_compare_fusion.3
  319.4 0.1 constant_dynamic-slice_fusion.2
  319.5 1.8 fusion.53
  321.4 1.2 multiply_subtract_fusion.2
  322.6 2.2 fusion.55
  324.7 2.3 pad_maximum_fusion.2
  327.1 11.3 %copy.20 = bf16[4096,256,2]{0,2,1:T(2,128)(2,1)} copy(bf16[4096,256,2]{1,0,2:T(8,128)(2,1)} %pad_maximum_fusion.2) | data formatting | bytes 8388608 | tf_op jit(solution)/shard_map/while/body/eval_jaxpr/stack | solution.py:40
  338.4 7.3 %convert_element_type.105 = bf16[4096,512]{0,1:T(8,128)(2,1)} reshape(bf16[4096,256,2]{0,2,1:T(2,128)(2,1)} %copy.20) | data formatting | bytes 8388608 | tf_op jit(solution)/shard_map/while/body/eval_jaxpr/convert_element_type | solution.py:42
  345.6 4.5 %fusion.56 = bf16[4,4096,128]{2,1,0:T(8,128)(2,1)} fusion(bf16[4,4096,128]{2,1,0:T(8,128)(2,1)} %get-tuple-element.199, s32[]{:T(128)S(6)} %copy.24, bf16[4096,512]{0,1:T(8,128)(2,1)} %convert_element_type.105, bf16[512,128]{1,0:T(8,128)(2,1)S(1)} %bitcast.76), kind=kOutput, calls=%fused_computation.2.clone.1 | convolution fusion | flops 537395200 | bytes 5373956 | tf_op jit(solution)/shard_map/while/body/eval_jaxpr/dot_general | solution.py:77
  350.1 1.6 copy-done.1
  (13 shorter events, 0.0 us)
Async XLA Ops:
  6.5 166.7 %copy-start = (bf16[16,1024,64]{1,2,0:T(8,128)(2,1)S(1)}, bf16[16,1024,64]{1,2,0:T(8,128)(2,1)}, u32[]{:S(2)}) copy-start(bf16[16,1024,64]{1,2,0:T(8,128)(2,1)} %param.13) | copy-start | bytes 6291460
  6.5 123.5 %all-gather.2.cloned.1.call-start = ((), (), s32[]{:S(2)}) async-start(), calls=%async_computation.1 | async-start | bytes 17825792 | tf_op jit(solution)/shard_map/all_gather | solution.py:54
  9.0 150.2 %copy-start.3 = (f32[128,128]{1,0:T(8,128)S(1)}, f32[128,128]{1,0:T(8,128)}, u32[]{:S(2)}) copy-start(f32[128,128]{1,0:T(8,128)} %param.11) | copy-start | bytes 196612
  173.3 28.4 %copy-start.2 = (s32[256]{0:T(256)S(1)}, s32[256]{0:T(256)}, u32[]{:S(2)}) copy-start(s32[256]{0:T(256)} %param.14) | copy-start | bytes 3076
  176.2 25.0 %all-to-all-start = ((bf16[16,64,2,128]{3,2,0,1:T(2,128)(2,1)}), bf16[16,64,2,128]{3,2,0,1:T(2,128)(2,1)S(1)}, u32[]{:S(2)}, u32[]{:S(2)}) async-start(bf16[16,64,2,128]{3,2,0,1:T(2,128)(2,1)} %copy.13), calls=%async_computation | async-start | bytes 1048576 | tf_op jit(solution)/shard_map/all_to_all | solution.py:66
  350.1 1.6 copy-start.1
Sparse Core Ops, SparseCore 0:
  9.8 120.0 all-gather.1
where the time goes:
time: 361 us; the launch traced here: 359 us
  waiting for transfers between devices  139 us (39%)
  local copies, waits for them, and re-layouts  86.1 us (24%)
  matrix products  62.7 us (17%)
  other arithmetic  33.3 us (9%)
  loops' own time  16.2 us (4%)
  between operations  13.5 us (4%)
  starting transfers between devices  7.7 us (2%)
    all_gather x1, waiting for transfers between devices, on_device(): whole = lax.all_gather(divergence, 'col', axis=2, tiled=True)  121 us
    another operation x4, local copies, waits for them, and re-layouts, cycle_basis(): jnp.stack([cosine, sine], axis=2).reshape(length, 2 * wavenumbers.shape[0])  45.2 us
    dot_general x1, matrix products, on_device(): jnp.einsum('kl,srln->srkn', analysis, whole, precision=lax.Precision.HIGH...  29.2 us
    convert_element_type x4, local copies, waits for them, and re-layouts, cycle_basis(): return jnp.stack([cosine, sine], axis=2).reshape(length, 2 * wavenumbers....  29 us
    dot_general x4, matrix products, synthesize(): jnp.dot(basis, values, preferred_element_type=jnp.float32)  17.9 us
    all_to_all x1, waiting for transfers between devices, on_device(): lax.all_to_all(field, 'wave', split_axis=1, concat_axis=0, tiled=True)  17.3 us
    another operation x1, loops' own time, on_device(): grid = lax.map(synthesize, jnp.arange(band_size, dtype=jnp.int32))  16.2 us
    dot_general x1, matrix products, on_device(): jnp.einsum('lk,srkn->srln', synthesis, modes * factor[None, None], precis...  14.1 us
  transfers between devices with their start and end apart: 2, of which 2 were waited for; matrix products, arithmetic and copies ran while one was open for 0% of the time, Pallas kernels for 0%

commit v1 on v0

v1 whole, which is shorter than its diff:
```python
import math

import jax
import jax.numpy as jnp
from jax import lax
from jax.experimental import pallas as pl
from jax.experimental.pallas import tpu as pltpu
from jax.sharding import PartitionSpec as P

MESH = pl.DeviceIdType.MESH
F32 = jnp.float32
BF16 = jnp.bfloat16
LON = 4096
WAVES = 16
SIDE = 4
ROUNDS = 4
MIB = 1 << 20


def iota(shape, dim):
    return lax.broadcasted_iota(jnp.int32, shape, dim)


def dot(a, b):
    return jnp.dot(a, b, preferred_element_type=F32)


def cos_sin(turn):
    quadrant = jnp.floor(turn + 0.5)
    x = (turn - quadrant) * (0.5 * math.pi)
    z = x * x
    s = x * (1.0 + z * (-1.0 / 6 + z * (1.0 / 120 + z * (-1.0 / 5040 + z * (1.0 / 362880)))))
    c = 1.0 + z * (-0.5 + z * (1.0 / 24 + z * (-1.0 / 720 + z * (1.0 / 40320))))
    odd = (quadrant == 1.0) | (quadrant == 3.0)
    cosine = jnp.where(odd, s, c)
    sine = jnp.where(odd, c, s)
    cosine = jnp.where((quadrant == 1.0) | (quadrant == 2.0), -cosine, cosine)
    sine = jnp.where((quadrant == 2.0) | (quadrant == 3.0), -sine, sine)
    return cosine, sine


def kernel(
    wn_s, cp_s, wn_v, div, analysis, synthesis, helm, leg_hbm, out_hbm,
    X, XE, leg, LP, AH, AL, SS, HM, C, CE, G32, G, F, ML, UA, VA, CB, SB, basis, acc, stage,
    p1_send, p1_recv, p2_send, p2_recv, xe_send, xe_recv, z_send, z_recv, leg_sem, out_sem,
):
    w = lax.axis_index("wave")
    col = lax.axis_index("col")
    cx, cy = col // SIDE, col % SIDE

    def wrap(v, n=SIDE):
        return lax.rem(v + n, n)

    first = (cx, cy)
    second = (cy, cx)

    def column(kind, d1, d2):
        return d1 * SIDE + d2 if kind == 0 else d2 * SIDE + d1

    def step_first(kind, by):
        return (w, column(kind, wrap(first[kind] + by), second[kind]))

    def step_second(kind, by):
        return (w, column(kind, first[kind], wrap(second[kind] + by)))

    barrier = pltpu.get_barrier_semaphore()
    for kind in range(2):
        for by in (-1, 1):
            pl.semaphore_signal(barrier, inc=1, device_id=step_first(kind, by), device_id_type=MESH)

    def greet(d, _):
        pl.semaphore_signal(
            barrier, inc=1, device_id=(lax.rem(w + d, WAVES), col), device_id_type=MESH
        )
        return 0

    lax.fori_loop(1, WAVES, greet, 0)
    leg_copy = pltpu.make_async_copy(leg_hbm, leg, leg_sem)
    leg_copy.start()

    def low_of(i):
        m = wn_s[w * 16 + 2 * i]
        return jnp.minimum(m, 1023 - m), jnp.where(m > 511, 1, 0)

    lanes = iota((16, 512), 1)
    tile_lane = iota((16, 128), 1)
    extra = jnp.zeros((16, 128), F32)
    for i in range(8):
        lo, swap = low_of(i)
        low = div[2 * i + swap].reshape(16, 1024)
        high = div[2 * i + 1 - swap].reshape(16, 1024)
        rolled = pltpu.roll(high[:, 512:], lo, 1)
        kind, rho = i % 2, i // 2
        own = X.at[kind, rho, second[kind], first[kind]]
        own[0] = jnp.where(lanes >= lo, low[:, :512], rolled).astype(BF16)
        own[1] = low[:, 512:].astype(BF16)
        moved = pltpu.roll(rolled[:, 384:], i + 1, 1)
        extra = jnp.where(tile_lane == i, moved, extra)
    XE[cy, cx] = extra.astype(BF16)

    pl.semaphore_wait(barrier, 4 + WAVES - 1)

    BULKS = ((0, 1), (1, 3))

    def send(src, dst, to, send_sem, recv_sem):
        return pltpu.make_async_remote_copy(
            src_ref=src, dst_ref=dst, send_sem=send_sem, recv_sem=recv_sem,
            device_id=to, device_id_type=MESH,
        )

    def p1(kind, bulk, which):
        at, size = BULKS[bulk]
        rs = pl.ds(at, size)
        d1, d2 = first[kind], second[kind]
        if which < 2:
            ref = X.at[kind, rs, d2, d1]
        elif which == 2:
            ref = X.at[kind, rs, d2, wrap(d1 - 1), 0]
        else:
            ref = X.at[kind, rs, d2, wrap(d1 + 1), 1]
        to = step_first(kind, 1 if which % 2 == 0 else -1)
        return send(ref, ref, to, p1_send.at[kind, bulk, which], p1_recv.at[kind, bulk, which])

    def p1_arrived(kind, bulk, which):
        at, size = BULKS[bulk]
        rs = pl.ds(at, size)
        d1, d2 = first[kind], second[kind]
        by = -1 if which % 2 == 0 else 1
        if which < 2:
            ref = X.at[kind, rs, d2, wrap(d1 + by)]
        else:
            ref = X.at[kind, rs, d2, wrap(d1 + 2), which - 2]
        send(ref, ref, step_first(kind, by), p1_send.at[kind, bulk, which],
             p1_recv.at[kind, bulk, which]).wait_recv()

    def p2(kind, rho, which):
        d2 = second[kind]
        if which < 2:
            ref = X.at[kind, rho, d2]
        elif which == 2:
            ref = X.at[kind, rho, wrap(d2 - 1), :, 0]
        else:
            ref = X.at[kind, rho, wrap(d2 + 1), :, 1]
        to = step_second(kind, 1 if which % 2 == 0 else -1)
        return send(ref, ref, to, p2_send.at[kind, rho, which], p2_recv.at[kind, rho, which])

    def p2_arrived(kind, rho, which):
        d2 = second[kind]
        by = -1 if which % 2 == 0 else 1
        if which < 2:
            ref = X.at[kind, rho, wrap(d2 + by)]
        else:
            ref = X.at[kind, rho, wrap(d2 + 2), :, which - 2]
        send(ref, ref, step_second(kind, by), p2_send.at[kind, rho, which],
             p2_recv.at[kind, rho, which]).wait_recv()

    def xe(which):
        ref = (XE.at[cy, cx], XE.at[cy, cx], XE.at[cy, wrap(cx - 1)],
               XE.at[cy], XE.at[cy], XE.at[wrap(cy - 1)])[which]
        by = -1 if which in (1, 4) else 1
        to = step_first(0, by) if which < 3 else step_second(0, by)
        return send(ref, ref, to, xe_send.at[which], xe_recv.at[which])

    def xe_arrived(which):
        ref = (XE.at[cy, wrap(cx - 1)], XE.at[cy, wrap(cx + 1)], XE.at[cy, wrap(cx + 2)],
               XE.at[wrap(cy - 1)], XE.at[wrap(cy + 1)], XE.at[wrap(cy + 2)])[which]
        by = 1 if which in (1, 4) else -1
        to = step_first(0, by) if which < 3 else step_second(0, by)
        send(ref, ref, to, xe_send.at[which], xe_recv.at[which]).wait_recv()

    for bulk in range(2):
        for which in range(2):
            for kind in range(2):
                p1(kind, bulk, which).start()
        if bulk == 0:
            xe(0).start()
            xe(1).start()

    a_full = analysis[...]
    a_hi = a_full.astype(BF16)
    a_lo = (a_full - a_hi.astype(F32)).astype(BF16)
    row = iota((128, 256), 0)
    j = iota((128, 256), 1)
    j2, j1 = j >> 6, (j >> 4) & 3
    for kind in range(2):
        level = (j1 * SIDE + j2 if kind == 0 else j2 * SIDE + j1) * 8 + (j & 7)
        for r in range(2):
            pick = jnp.where((row == level) & (((j >> 3) & 1) == r), 1.0, 0.0).astype(BF16)
            AH[kind, r * 128:(r + 1) * 128] = dot(a_hi, pick).astype(BF16)
            AL[kind, r * 128:(r + 1) * 128] = dot(a_lo, pick).astype(BF16)
    s_full = synthesis[...]
    s_hi = s_full.astype(BF16)
    SS[:, 0:128] = s_hi
    SS[:, 128:256] = (s_full - s_hi.astype(F32)).astype(BF16)
    h_rows = jnp.broadcast_to(helm[...], (128, 128)).T
    for q in range(4):
        HM[:, q * 128:(q + 1) * 128] = h_rows

    lane = iota((256, 512), 1)
    slot = ((lane >> 3) & 15) * 16 + 4 * (lane >> 7) + 2 * ((lane >> 1) & 1)
    choose = jnp.where(iota((256, 512), 0) == slot, 1.0, 0.0).astype(BF16)
    wn = jnp.broadcast_to(wn_v[...], (16, 256))
    upper = dot((wn >> 5).astype(F32).astype(BF16), choose)
    lower = dot((wn & 31).astype(F32).astype(BF16), choose)
    m0 = (upper * 32.0 + lower)[0:8]
    m_lo = jnp.minimum(m0, 1023.0 - m0)
    ML[...] = jnp.where((iota((8, 512), 1) & 1) == 1, 1023.0 - m_lo, m_lo)

    for kind in range(2):
        for which in range(2):
            p1_arrived(kind, 0, which)
            p1(kind, 0, 2 + which).start()
    xe_arrived(0)
    xe(2).start()
    xe_arrived(1)

    leg_copy.wait()

    def leg_pack(i, _):
        lo, swap = low_of(i)
        low = leg.at[2 * i + swap]
        high = leg.at[2 * i + 1 - swap]
        p = iota((64, 512), 1)
        rolled = pltpu.roll(high[:, 512:].astype(F32), lo, 1)
        LP[i, 0:64, 0:512] = jnp.where(p >= lo, low[:, 0:512].astype(F32), 0.0).astype(BF16)
        LP[i, 64:128, 0:512] = jnp.where(p < lo, rolled, 0.0).astype(BF16)
        LP[i, 0:64, 512:1024] = low[:, 512:]
        LP[i, 64:128, 512:1024] = jnp.zeros((64, 512), BF16)
        LP[i, 0:64, 1024:1152] = jnp.zeros((64, 128), BF16)
        moved = pltpu.roll(rolled[:, 384:], i + 1, 1)
        LP[i, 64:128, 1024:1152] = jnp.where(iota((64, 128), 1) == i, moved, 0.0).astype(BF16)
        return 0

    for kind in range(2):
        for which in range(2):
            p1_arrived(kind, 0, 2 + which)
    for which in range(2):
        for kind in range(2):
            p2(kind, 0, which).start()
    for kind in range(2):
        for which in range(2):
            p1_arrived(kind, 1, which)
            p1(kind, 1, 2 + which).start()
    lax.fori_loop(0, 4, leg_pack, 0)
    xe_arrived(2)
    xe(3).start()
    xe(4).start()
    for kind in range(2):
        for which in range(2):
            p1_arrived(kind, 1, 2 + which)
    for which in range(2):
        for kind in range(2):
            p2(kind, 1, which).start()
    xe_arrived(3)
    xe(5).start()
    lax.fori_loop(4, 8, leg_pack, 0)

    def make_angles(u):
        latitude = col * 64 + w * 4 + u
        points = jnp.full((64, 512), cp_s[latitude], jnp.int32).astype(F32)
        inverse = 1.0 / points
        m = jnp.broadcast_to(ML[0:1], (64, 512))
        index = iota((64, 512), 0).astype(F32)
        lane = iota((64, 512), 1)
        imaginary = ((lane >> 2) & 1) == 1
        weight = jnp.where(m == 0.0, 1.0, 2.0) / math.sqrt(256.0)

        def angle(product):
            rest = product - jnp.floor(product * inverse) * points
            rest = jnp.where(rest < 0.0, rest + points, rest)
            rest = jnp.where(rest >= points, rest - points, rest)
            return cos_sin(rest * (4.0 * inverse))

        c, s = angle(index * 64.0 * m)
        c, s = weight * c, -weight * s
        UA[...] = jnp.where(imaginary, s, c)
        VA[...] = jnp.where(imaginary, -c, s)
        c, s = angle(index * m)
        CB[...] = c
        SB[...] = s

    def make_basis(u):
        def rows(a8, _):
            some = pl.ds(pl.multiple_of(a8 * 8, 8), 8)
            for q in range(4):
                at = pl.ds(q * 128, 128)
                ua, va, cb, sb = UA[some, at], VA[some, at], CB[:, at], SB[:, at]
                for k in range(8):
                    value = ua[k:k + 1] * cb + va[k:k + 1] * sb
                    start = pl.multiple_of(a8 * 512, 512) + k * 64
                    basis[u, pl.ds(start, 64), at] = value.astype(BF16)
            return 0

        lax.fori_loop(0, 8, rows, 0)

    def solve(x, kind, n, count):
        modes = dot(AH[kind], x) + dot(AL[kind], x)
        factor = 1.0 / (1.0 + HM[:, 0:count] * (n * (n + 1.0)))
        out = []
        for r in range(2):
            part = modes[r * 128:(r + 1) * 128] * factor
            hi = part.astype(BF16)
            lo = (part - hi.astype(F32)).astype(BF16)
            both = jnp.concatenate([hi, hi], axis=0)
            out.append((dot(SS[...], both) + dot(SS[:, 0:128], lo)).astype(BF16))
        return out

    def field(kind, rho):
        i = 2 * rho + kind
        lo, _ = low_of(i)
        for h in range(2):
            p = iota((1, 512), 1) + h * 512
            n = jnp.where(p >= lo, p, p + 1024 - lo).astype(F32)
            x = X[kind, rho, :, :, h].reshape(256, 512)
            out = solve(x, kind, n, 512)
            for r in range(2):
                C[r * 128:(r + 1) * 128, h * 512:(h + 1) * 512] = out[r]
        contract = (((1,), (1,)), ((), ()))
        total = lax.dot_general(LP[i, :, 0:1024], C[...], contract, preferred_element_type=F32)
        total += lax.dot_general(LP[i, :, 1024:1152], CE[...], contract, preferred_element_type=F32)
        for r in range(2):
            for side in range(2):
                G32[pl.ds(r * 4 + kind * 2 + side, 64, stride=8)] = (
                    total[side * 64:(side + 1) * 64, r * 128:(r + 1) * 128]
                )

    def z_copy(rho, d):
        to = lax.rem(w + d, WAVES)
        return send(G.at[rho, to], F.at[rho, w], (to, col), z_send.at[rho, d], z_recv.at[rho, d])

    def z_start(rho):
        G[rho] = G32[...].reshape(WAVES, 2, 16, 128).astype(BF16)

        def one(d, _):
            z_copy(rho, d).start()
            return 0

        lax.fori_loop(1, WAVES, one, 0)
        F[rho, w] = G[rho, w]

    def z_wait(rho):
        def one(d, _):
            come = lax.rem(w - d + WAVES, WAVES)
            send(G.at[rho, come], F.at[rho, come], (come, col), z_send.at[rho, d],
                 z_recv.at[rho, d]).wait_recv()
            return 0

        lax.fori_loop(1, WAVES, one, 0)

    def grid(u, g):
        parts = []
        for rho in (2 * g, 2 * g + 1):
            tiles = F[rho, :, u // 2].astype(F32)
            at = (u % 2) * 8
            parts.append(tiles[:, at:at + 8].reshape(128, 128))
        values = jnp.concatenate(parts, axis=0).astype(BF16)
        points = cp_s[col * 64 + w * 4 + u]

        def rows(k, _):
            at = pl.ds(pl.multiple_of(k * 512, 512), 512)
            part = dot(basis[u, at, g * 256:(g + 1) * 256], values)
            if g == 0:
                acc[u, at] = part
            else:
                live = iota((512, 128), 0) + k * 512 < points
                stage[u, at] = jnp.where(live, acc[u, at] + part, 0.0).astype(BF16)
            return 0

        lax.fori_loop(0, LON // 512, rows, 0)

    def out_copy(u):
        return pltpu.make_async_copy(stage.at[u], out_hbm.at[0, u], out_sem.at[u])

    for rho in range(ROUNDS):
        for kind in range(2):
            for which in range(2):
                p2_arrived(kind, rho, which)
                p2(kind, rho, 2 + which).start()
        if rho < 2:
            for which in range(2):
                for kind in range(2):
                    p2(kind, rho + 2, which).start()
        if rho < 2:
            for u in (2 * rho, 2 * rho + 1):
                make_angles(u)
                make_basis(u)
        else:
            if rho == 2:
                z_wait(0)
                z_wait(1)
            for u in (2 * rho - 4, 2 * rho - 3):
                grid(u, 0)
        if rho == 0:
            xe_arrived(4)
            xe_arrived(5)
            n = jnp.zeros((1, 128), F32)
            for i in range(8):
                lo, _ = low_of(i)
                n = jnp.where(iota((1, 128), 1) == i, (1023 - lo).astype(F32), n)
            out = solve(XE[...].reshape(256, 128), 0, n, 128)
            for r in range(2):
                CE[r * 128:(r + 1) * 128] = out[r]
        for kind in range(2):
            for which in range(2):
                p2_arrived(kind, rho, 2 + which)
            field(kind, rho)
        z_start(rho)

    for kind in range(2):
        for which in range(4):
            for bulk in range(2):
                p1(kind, bulk, which).wait_send()
            for rho in range(ROUNDS):
                p2(kind, rho, which).wait_send()
    for which in range(6):
        xe(which).wait_send()
    z_wait(2)
    z_wait(3)
    for u in range(4):
        grid(u, 1)
        out_copy(u).start()
    for rho in range(ROUNDS):
        def sent(d, _, rho=rho):
            z_copy(rho, d).wait_send()
            return 0

        lax.fori_loop(1, WAVES, sent, 0)
    for u in range(4):
        out_copy(u).wait()


def on_device(divergence, analysis, synthesis, helmholtz, legendre, wavenumbers, cycle_points):
    vmem = pl.BlockSpec(memory_space=pltpu.VMEM)
    smem = pl.BlockSpec(memory_space=pltpu.SMEM)
    hbm = pl.BlockSpec(memory_space=pl.ANY)
    dma = pltpu.SemaphoreType.DMA
    return pl.pallas_call(
        kernel,
        out_shape=jax.ShapeDtypeStruct((1, 4, LON, 128), BF16),
        in_specs=[smem, smem, vmem, vmem, vmem, vmem, vmem, hbm],
        out_specs=hbm,
        scratch_shapes=[
            pltpu.VMEM((2, ROUNDS, SIDE, SIDE, 2, 16, 512), BF16),
            pltpu.VMEM((SIDE, SIDE, 16, 128), BF16),
            pltpu.VMEM((16, 64, 1024), BF16),
            pltpu.VMEM((8, 128, 1152), BF16),
            pltpu.VMEM((2, 256, 256), BF16),
            pltpu.VMEM((2, 256, 256), BF16),
            pltpu.VMEM((128, 256), BF16),
            pltpu.VMEM((128, 512), F32),
            pltpu.VMEM((256, 1024), BF16),
            pltpu.VMEM((256, 128), BF16),
            pltpu.VMEM((512, 128), F32),
            pltpu.VMEM((ROUNDS, WAVES, 2, 16, 128), BF16),
            pltpu.VMEM((ROUNDS, WAVES, 2, 16, 128), BF16),
            pltpu.VMEM((8, 512), F32),
            pltpu.VMEM((64, 512), F32),
            pltpu.VMEM((64, 512), F32),
            pltpu.VMEM((64, 512), F32),
            pltpu.VMEM((64, 512), F32),
            pltpu.VMEM((4, LON, 512), BF16),
            pltpu.VMEM((4, LON, 128), F32),
            pltpu.VMEM((4, LON, 128), BF16),
            dma((2, 2, 4)), dma((2, 2, 4)),
            dma((2, ROUNDS, 4)), dma((2, ROUNDS, 4)),
            dma((6,)), dma((6,)),
            dma((ROUNDS, WAVES)), dma((ROUNDS, WAVES)),
            dma(()), dma((4,)),
        ],
        compiler_params=pltpu.CompilerParams(
            collective_id=0, has_side_effects=True, vmem_limit_bytes=58 * MIB
        ),
        cost_estimate=pl.CostEstimate(flops=6 << 30, bytes_accessed=8 * MIB, transcendentals=0),
    )(
        wavenumbers, cycle_points, wavenumbers.reshape(1, 256), divergence, analysis, synthesis,
        helmholtz.reshape(1, 128), jnp.swapaxes(legendre, 1, 2),
    )


def solution(mesh):
    placed = (P("wave", None, "col", None), P(), P(), P(), P("wave", None, "col"), P(), P())
    return jax.shard_map(
        on_device,
        mesh=mesh,
        in_specs=placed,
        out_specs=P("col", "wave", None, None),
        check_vma=False,
    )
```

time: 361 us -> 81.6 us (0.23)
  waiting for transfers between devices: 139 us -> 0 us
  local copies, waits for them, and re-layouts: 86.1 us -> 4.47 us
  Pallas kernels: 0 us -> 77 us
  matrix products: 62.7 us -> 0 us
  other arithmetic: 33.3 us -> 0 us
  loops' own time: 16.2 us -> 0 us
  between operations: 13.5 us -> 0.01 us
  starting transfers between devices: 7.7 us -> 0 us
    all_gather x1 -> x0, waiting for transfers between devices: 121 us -> none  [on_device(): whole = lax.all_gather(divergence, 'col', axis=2, tiled=True)]
    pallas_call x0 -> x1, Pallas kernels: none -> 77 us  [on_device(): pl.pallas_call(kernel, out_shape=jax.ShapeDtypeStruct((1, 4, LON, 128), B...]
    dot_general x7 -> x0, matrix products: 62.7 us -> none  [the longest x1 29.2 us: on_device(): jnp.einsum('kl,srln->srkn', analysis, whole, precision=lax.Precision.HIGH...]
    another operation x4 -> x0, local copies, waits for them, and re-layouts: 45.2 us -> none  [cycle_basis(): jnp.stack([cosine, sine], axis=2).reshape(length, 2 * wavenumbers.shape[0])]
    convert_element_type x5 -> x0, local copies, waits for them, and re-layouts: 30.3 us -> none  [the longest x4 29 us: cycle_basis(): return jnp.stack([cosine, sine], axis=2).reshape(length, 2 * wavenumbers....]
    another operation x8 -> x0, other arithmetic: 18 us -> none  [the longest x4 9.35 us: cycle_basis(): jnp.stack([cosine, sine], axis=2).reshape(length, 2 * wavenumbers.shape[0])]
    all_to_all x1 -> x0, waiting for transfers between devices: 17.3 us -> none  [on_device(): lax.all_to_all(field, 'wave', split_axis=1, concat_axis=0, tiled=True)]
    another operation x1 -> x0, loops' own time: 16.2 us -> none  [on_device(): grid = lax.map(synthesize, jnp.arange(band_size, dtype=jnp.int32))]
  transfers between devices with their start and end apart: 2 -> 0, of which waited for: 2 -> 0; matrix products, arithmetic and copies ran while one was open for 0% -> 0% of each run, Pallas kernels for 0% -> 0%
where the time goes in v1:
time: 81.6 us; the launch traced here: 81.5 us
  Pallas kernels  77 us (94%)
  local copies, waits for them, and re-layouts  4.47 us (5%)
    pallas_call x1, Pallas kernels, on_device(): pl.pallas_call(kernel, out_shape=jax.ShapeDtypeStruct((1, 4, LON, 128), B...  77 us
    unnamed x1, local copies, waits for them, and re-layouts  4.47 us

profile of v1, /device:TPU:1, one launch (start us, length us, event | category | flops | bytes accessed | tf_op | source)
XLA Modules:
  0.0 81.5 jit_solution(13937591045850733980)
XLA Ops:
  0.0 77.0 %shard_map.73 = bf16[1,4,4096,128]{3,2,1,0:T(8,128)(2,1)} custom-call(s32[256]{0:T(256)} %wn_s.1, s32[1024]{0:T(1024)} %cp_s.1, s32[1,256]{1,0:T(1,128)} %bitcast.4, f32[16,2,8,1024]{3,2,1,0:T(8,128)} %div.1, f32[128,128]{1,0:T(8,128)} %analysis.1, f32[128,128]{1,0:T(8,128)} %synthesis.1, f32[1,128]{1,0:T(1,128)} %bitcast.5, bf16[16,64,1024]{2,1,0:T(8,128)(2,1)} %bitcast.3), custom_call_target="tpu_custom_call" | custom-call | flops 6442450944 | bytes 8388608 | tf_op jit(solution)/shard_map/pallas_call | solution.py:437
  77.0 4.5 %copy.9 = bf16[1,4,4096,128]{3,2,1,0:T(8,128)(2,1)} copy(bf16[1,4,4096,128]{3,2,1,0:T(8,128)(2,1)} %shard_map.73) | data formatting | bytes 8388608

commit v2 on v1

v2 whole, which is shorter than its diff:
```python
import math

import jax
import jax.numpy as jnp
from jax import lax
from jax.experimental import pallas as pl
from jax.experimental.pallas import tpu as pltpu
from jax.sharding import PartitionSpec as P

MESH = pl.DeviceIdType.MESH
F32 = jnp.float32
BF16 = jnp.bfloat16
LON = 4096
WAVES = 16
HALF = LON // 2
SIDE = 4
ROUNDS = 4
BEFORE = 2
MIB = 1 << 20


def iota(shape, dim):
    return lax.broadcasted_iota(jnp.int32, shape, dim)


def dot(a, b):
    return jnp.dot(a, b, preferred_element_type=F32)


def cos_sin(turn):
    quadrant = jnp.floor(turn + 0.5)
    x = (turn - quadrant) * (0.5 * math.pi)
    z = x * x
    s = x * (1.0 + z * (-1.0 / 6 + z * (1.0 / 120 + z * (-1.0 / 5040 + z * (1.0 / 362880)))))
    c = 1.0 + z * (-0.5 + z * (1.0 / 24 + z * (-1.0 / 720 + z * (1.0 / 40320))))
    odd = (quadrant == 1.0) | (quadrant == 3.0)
    cosine = jnp.where(odd, s, c)
    sine = jnp.where(odd, c, s)
    cosine = jnp.where((quadrant == 1.0) | (quadrant == 2.0), -cosine, cosine)
    sine = jnp.where((quadrant == 2.0) | (quadrant == 3.0), -sine, sine)
    return cosine, sine


def gather_kernel(
    wn_s, cp_s, wn_v, div, analysis, synthesis, helm, leg_hbm, basis_hbm, values_hbm,
    X, XE, leg, LP, AHL, SS, HM, C, CE, G32, G, F, ML, SG, UA, VA, CB, SB, basis, V,
    p1_send, p1_recv, p2_send, p2_recv, xe_send, xe_recv, z_send, z_recv,
    leg_sem, basis_sem, values_sem,
):
    w = lax.axis_index("wave")
    col = lax.axis_index("col")
    cx, cy = col // SIDE, col % SIDE

    def wrap(v, n=SIDE):
        return lax.rem(v + n, n)

    first = (cx, cy)
    second = (cy, cx)

    def column(kind, d1, d2):
        return d1 * SIDE + d2 if kind == 0 else d2 * SIDE + d1

    def step_first(kind, by):
        return (w, column(kind, wrap(first[kind] + by), second[kind]))

    def step_second(kind, by):
        return (w, column(kind, first[kind], wrap(second[kind] + by)))

    barrier = pltpu.get_barrier_semaphore()
    for kind in range(2):
        for by in (1, 2, 3):
            pl.semaphore_signal(barrier, inc=1, device_id=step_first(kind, by), device_id_type=MESH)

    def greet(d, _):
        pl.semaphore_signal(
            barrier, inc=1, device_id=(lax.rem(w + d, WAVES), col), device_id_type=MESH
        )
        return 0

    lax.fori_loop(1, WAVES, greet, 0)
    leg_copy = pltpu.make_async_copy(leg_hbm, leg, leg_sem)
    leg_copy.start()

    def low_of(i):
        m = wn_s[w * 16 + 2 * i]
        return jnp.minimum(m, 1023 - m), jnp.where(m > 511, 1, 0)

    lanes = iota((16, 512), 1)
    tile_lane = iota((16, 128), 1)
    extra = jnp.zeros((16, 128), F32)
    for i in range(8):
        lo, swap = low_of(i)
        low = div[2 * i + swap].reshape(16, 1024)
        high = div[2 * i + 1 - swap].reshape(16, 1024)
        rolled = pltpu.roll(high[:, 512:], lo, 1)
        kind, rho = i % 2, i // 2
        own = X.at[kind, rho, second[kind], first[kind]]
        own[0] = jnp.where(lanes >= lo, low[:, :512], rolled).astype(BF16)
        own[1] = low[:, 512:].astype(BF16)
        moved = pltpu.roll(rolled[:, 384:], i + 1, 1)
        extra = jnp.where(tile_lane == i, moved, extra)
    XE[cy, cx] = extra.astype(BF16)

    a_full = analysis[...]
    a_hi = a_full.astype(BF16)
    a_lo = (a_full - a_hi.astype(F32)).astype(BF16)
    row = iota((128, 256), 0)
    j = iota((128, 256), 1)
    j2, j1 = j >> 6, (j >> 4) & 3
    for kind in range(2):
        level = (j1 * SIDE + j2 if kind == 0 else j2 * SIDE + j1) * 8 + (j & 7)
        for r in range(2):
            pick = jnp.where((row == level) & (((j >> 3) & 1) == r), 1.0, 0.0).astype(BF16)
            AHL[kind, r * 128:(r + 1) * 128] = dot(a_hi, pick).astype(BF16)
            AHL[kind, 256 + r * 128:256 + (r + 1) * 128] = dot(a_lo, pick).astype(BF16)
    s_full = synthesis[...]
    s_hi = s_full.astype(BF16)
    SS[:, 0:128] = s_hi
    SS[:, 128:256] = (s_full - s_hi.astype(F32)).astype(BF16)
    h_rows = jnp.broadcast_to(helm[...], (128, 128)).T
    for q in range(4):
        HM[:, q * 128:(q + 1) * 128] = h_rows

    lane = iota((256, 512), 1)
    slot = ((lane >> 3) & 15) * 16 + 4 * (lane >> 7) + 2 * ((lane >> 1) & 1)
    choose = jnp.where(iota((256, 512), 0) == slot, 1.0, 0.0).astype(BF16)
    wn = jnp.broadcast_to(wn_v[...], (16, 256))
    upper = dot((wn >> 5).astype(F32).astype(BF16), choose)
    lower = dot((wn & 31).astype(F32).astype(BF16), choose)
    m0 = (upper * 32.0 + lower)[0:8]
    m_lo = jnp.minimum(m0, 1023.0 - m0)
    m_lane = jnp.where((iota((8, 512), 1) & 1) == 1, 1023.0 - m_lo, m_lo)
    ML[...] = m_lane
    sign = 1.0 - 2.0 * (m_lane - 2.0 * jnp.floor(m_lane * 0.5))
    for q in range(4):
        part = jnp.broadcast_to(sign[0:1, q * 128:(q + 1) * 128], (128, 128))
        SG[q * 128:(q + 1) * 128] = part.T

    def make_angles(u):
        latitude = col * 64 + w * 4 + u

        def angle(index, count):
            points = jnp.full((count, 512), cp_s[latitude], jnp.int32).astype(F32)
            inverse = 1.0 / points
            product = index.astype(F32) * jnp.broadcast_to(ML[0:1], (count, 512))
            rest = product - jnp.floor(product * inverse) * points
            rest = jnp.where(rest < 0.0, rest + points, rest)
            rest = jnp.where(rest >= points, rest - points, rest)
            return cos_sin(rest * (4.0 * inverse))

        c, s = angle(iota((32, 512), 0) * 64, 32)
        weight = jnp.where(ML[0:1] == 0.0, 1.0, 2.0) / math.sqrt(256.0)
        imaginary = ((iota((32, 512), 1) >> 2) & 1) == 1
        c, s = weight * c, -weight * s
        UA[...] = jnp.where(imaginary, s, c)
        VA[...] = jnp.where(imaginary, -c, s)
        c, s = angle(iota((64, 512), 0), 64)
        CB[...] = c
        SB[...] = s

    def basis_copy(u):
        return pltpu.make_async_copy(basis.at[u], basis_hbm.at[u], basis_sem.at[u])

    def make_basis(u, _):
        make_angles(u)

        def rows(a8, _):
            some = pl.ds(pl.multiple_of(a8 * 8, 8), 8)
            for q in range(4):
                at = pl.ds(q * 128, 128)
                ua, va, cb, sb = UA[some, at], VA[some, at], CB[:, at], SB[:, at]
                for k in range(8):
                    value = ua[k:k + 1] * cb + va[k:k + 1] * sb
                    start = pl.multiple_of(a8 * 512, 512) + k * 64
                    basis[u, pl.ds(start, 64), at] = value.astype(BF16)
            return 0

        lax.fori_loop(0, HALF // 512, rows, 0)
        basis_copy(u).start()
        return 0

    lax.fori_loop(0, BEFORE, make_basis, 0)
    pl.semaphore_wait(barrier, 6 + WAVES - 1)

    BULKS = ((0, 1), (1, 1), (2, 2))

    def send(src, dst, to, send_sem, recv_sem):
        return pltpu.make_async_remote_copy(
            src_ref=src, dst_ref=dst, send_sem=send_sem, recv_sem=recv_sem,
            device_id=to, device_id_type=MESH,
        )

    def bytes_of(ref, send_sem, recv_sem):
        return send(ref, ref, step_first(0, 1), send_sem, recv_sem)

    def p1_start(kind, bulk):
        at, size = BULKS[bulk]
        ref = X.at[kind, pl.ds(at, size), second[kind], first[kind]]
        for by in (2, 1, 3):
            send(ref, ref, step_first(kind, by), p1_send.at[kind, bulk], p1_recv.at[kind, bulk]).start()

    def p1_all(kind, bulk):
        at, size = BULKS[bulk]
        ref = X.at[kind, pl.ds(at, size), second[kind], pl.ds(0, 3)]
        return bytes_of(ref, p1_send.at[kind, bulk], p1_recv.at[kind, bulk])

    def p2(kind, rho, which):
        d2 = second[kind]
        if which < 2:
            ref = X.at[kind, rho, d2]
        elif which == 2:
            ref = X.at[kind, rho, wrap(d2 - 1), :, 0]
        else:
            ref = X.at[kind, rho, wrap(d2 + 1), :, 1]
        to = step_second(kind, 1 if which % 2 == 0 else -1)
        return send(ref, ref, to, p2_send.at[kind, rho], p2_recv.at[kind, rho, min(which, 2)])

    def p2_direct(rho):
        for which in range(2):
            for kind in range(2):
                p2(kind, rho, which).start()

    def p2_row(kind, rho, which):
        ref = X.at[kind, rho, wrap(second[kind] + (-1 if which == 0 else 1))]
        bytes_of(ref, p2_send.at[kind, rho], p2_recv.at[kind, rho, which]).wait_recv()

    def p2_relayed(kind, rho):
        ref = X.at[kind, rho, wrap(second[kind] + 2)]
        bytes_of(ref, p2_send.at[kind, rho], p2_recv.at[kind, rho, 2]).wait_recv()

    def xe_start(stage):
        ref = XE.at[cy, cx] if stage == 0 else XE.at[cy]
        for by in (2, 1, 3):
            to = step_first(0, by) if stage == 0 else step_second(0, by)
            send(ref, ref, to, xe_send.at[stage], xe_recv.at[stage]).start()

    def xe_all(stage):
        ref = XE.at[cy, pl.ds(0, 3)] if stage == 0 else XE.at[pl.ds(0, 3)]
        return bytes_of(ref, xe_send.at[stage], xe_recv.at[stage])

    for bulk in range(3):
        for kind in range(2):
            p1_start(kind, bulk)
        if bulk == 0:
            xe_start(0)

    lax.fori_loop(BEFORE, BEFORE + 1, make_basis, 0)
    leg_copy.wait()

    def leg_pack(i, _):
        lo, swap = low_of(i)
        low = leg.at[2 * i + swap]
        high = leg.at[2 * i + 1 - swap]
        p = iota((64, 512), 1)
        rolled = pltpu.roll(high[:, 512:].astype(F32), lo, 1)
        LP[i, 0:64, 0:512] = jnp.where(p >= lo, low[:, 0:512].astype(F32), 0.0).astype(BF16)
        LP[i, 64:128, 0:512] = jnp.where(p < lo, rolled, 0.0).astype(BF16)
        LP[i, 0:64, 512:1024] = low[:, 512:]
        LP[i, 64:128, 512:1024] = jnp.zeros((64, 512), BF16)
        LP[i, 0:64, 1024:1152] = jnp.zeros((64, 128), BF16)
        moved = pltpu.roll(rolled[:, 384:], i + 1, 1)
        LP[i, 64:128, 1024:1152] = jnp.where(iota((64, 128), 1) == i, moved, 0.0).astype(BF16)
        return 0

    for kind in range(2):
        p1_all(kind, 0).wait_recv()
    p2_direct(0)
    xe_all(0).wait_recv()
    xe_start(1)
    lax.fori_loop(0, 4, leg_pack, 0)
    for kind in range(2):
        p1_all(kind, 1).wait_recv()
    p2_direct(1)
    lax.fori_loop(4, 8, leg_pack, 0)
    for kind in range(2):
        p1_all(kind, 2).wait_recv()

    def solve(x, kind, n, count):
        modes = dot(AHL[kind], x)
        modes = modes[0:256] + modes[256:512]
        factor = 1.0 / (1.0 + HM[:, 0:count] * (n * (n + 1.0)))
        out = []
        for r in range(2):
            part = modes[r * 128:(r + 1) * 128] * factor
            hi = part.astype(BF16)
            lo = (part - hi.astype(F32)).astype(BF16)
            both = jnp.concatenate([hi, hi], axis=0)
            out.append((dot(SS[...], both) + dot(SS[:, 0:128], lo)).astype(BF16))
        return out

    def field(kind, rho):
        i = 2 * rho + kind
        lo, _ = low_of(i)
        for h in range(2):
            p = iota((1, 512), 1) + h * 512
            n = jnp.where(p >= lo, p, p + 1024 - lo).astype(F32)
            x = X[kind, rho, :, :, h].reshape(256, 512)
            out = solve(x, kind, n, 512)
            for r in range(2):
                C[r * 128:(r + 1) * 128, h * 512:(h + 1) * 512] = out[r]
        contract = (((1,), (1,)), ((), ()))
        total = lax.dot_general(LP[i, :, 0:1024], C[...], contract, preferred_element_type=F32)
        total += lax.dot_general(LP[i, :, 1024:1152], CE[...], contract, preferred_element_type=F32)
        for r in range(2):
            for side in range(2):
                G32[pl.ds(r * 4 + kind * 2 + side, 64, stride=8)] = (
                    total[side * 64:(side + 1) * 64, r * 128:(r + 1) * 128]
                )

    def z_start(rho):
        G[rho] = G32[...].reshape(WAVES, 2, 16, 128).astype(BF16)

        def one(d, _):
            to = lax.rem(w + d, WAVES)
            send(G.at[rho, to], F.at[rho, w], (to, col), z_send.at[rho], z_recv.at[rho]).start()
            return 0

        lax.fori_loop(1, WAVES, one, 0)
        F[rho, w] = G[rho, w]

    def z_all(rho):
        return bytes_of(F.at[rho, pl.ds(0, WAVES - 1)], z_send.at[rho], z_recv.at[rho])

    def values_copy(rho):
        return pltpu.make_async_copy(V.at[rho], values_hbm.at[rho], values_sem.at[rho])

    def make_values(rho):
        z_all(rho).wait_recv()
        sign = SG[rho * 128:(rho + 1) * 128]
        for u in range(4):
            tiles = F[rho, :, u // 2].astype(F32)
            at = (u % 2) * 8
            part = tiles[:, at:at + 8].reshape(128, 128)
            V[rho, u, :, 0:128] = part.astype(BF16)
            V[rho, u, :, 128:256] = (part * sign).astype(BF16)
        values_copy(rho).start()

    for rho in range(ROUNDS):
        for kind in range(2):
            for which in range(2):
                p2_row(kind, rho, which)
                p2(kind, rho, 2 + which).start()
        if rho < 2:
            p2_direct(rho + 2)
        if rho == 0:
            lax.fori_loop(BEFORE + 1, 4, make_basis, 0)
            xe_all(1).wait_recv()
            n = jnp.zeros((1, 128), F32)
            for i in range(8):
                lo, _ = low_of(i)
                n = jnp.where(iota((1, 128), 1) == i, (1023 - lo).astype(F32), n)
            out = solve(XE[...].reshape(256, 128), 0, n, 128)
            for r in range(2):
                CE[r * 128:(r + 1) * 128] = out[r]
        if rho >= 2:
            make_values(rho - 2)
        for kind in range(2):
            p2_relayed(kind, rho)
            field(kind, rho)
        z_start(rho)

    for kind in range(2):
        for bulk in range(3):
            p1_all(kind, bulk).wait_send()
        for rho in range(ROUNDS):
            ref = X.at[kind, rho, pl.ds(0, 3)]
            bytes_of(ref, p2_send.at[kind, rho], p2_recv.at[kind, rho, 0]).wait_send()
    for stage in range(2):
        xe_all(stage).wait_send()
    for u in range(4):
        basis_copy(u).wait()
    make_values(2)
    make_values(3)
    for rho in range(ROUNDS):
        z_all(rho).wait_send()
        values_copy(rho).wait()


def grid_kernel(cp_s, basis_hbm, values_hbm, out_hbm, basis, V, D, stage, basis_sem, values_sem, out_sem):
    first = lax.axis_index("col") * 64 + lax.axis_index("wave") * 4

    def basis_copy(u, b):
        at = pl.ds(b * 1024, 1024)
        return pltpu.make_async_copy(basis_hbm.at[u, at], basis.at[u, at], basis_sem.at[u, b])

    def values_copy(u):
        return pltpu.make_async_copy(values_hbm.at[:, u], V.at[u], values_sem.at[u])

    def out_copy(u, b):
        at = pl.ds(b * HALF, HALF)
        return pltpu.make_async_copy(stage.at[u, at], out_hbm.at[0, u, at], out_sem.at[u, b])

    for u in range(4):
        values_copy(u).start()
        for b in range(2):
            basis_copy(u, b).start()
    for u in range(4):
        points = cp_s[first + u]
        half = points >> 1
        values_copy(u).wait()
        values = V[u].reshape(512, 256)

        def turned(at):
            return D[pl.ds(pl.multiple_of(1024 + at - half, 8), 512)]

        for b in range(2):
            basis_copy(u, b).wait()
            both = dot(basis[u, b * 1024:(b + 1) * 1024], values)
            D[1024 + b * 1024:2048 + b * 1024] = both[:, 128:256]
            plus = both[:, 0:128]
            if b == 0:
                stage[u, 0:1024] = plus.astype(BF16)
            else:
                for k in range(2):
                    at = 1024 + k * 512
                    j = iota((512, 128), 0) + at
                    here = plus[k * 512:(k + 1) * 512]
                    stage[u, at:at + 512] = jnp.where(j < half, here, turned(at)).astype(BF16)
        out_copy(u, 0).start()
        for k in range(4):
            at = HALF + k * 512
            j = iota((512, 128), 0) + at
            stage[u, at:at + 512] = jnp.where(j < points, turned(at), 0.0).astype(BF16)
        out_copy(u, 1).start()
    for u in range(4):
        for b in range(2):
            out_copy(u, b).wait()


def on_device(divergence, analysis, synthesis, helmholtz, legendre, wavenumbers, cycle_points):
    vmem = pl.BlockSpec(memory_space=pltpu.VMEM)
    smem = pl.BlockSpec(memory_space=pltpu.SMEM)
    hbm = pl.BlockSpec(memory_space=pl.ANY)
    dma = pltpu.SemaphoreType.DMA
    basis, values = pl.pallas_call(
        gather_kernel,
        out_shape=(
            jax.ShapeDtypeStruct((4, HALF, 512), BF16),
            jax.ShapeDtypeStruct((ROUNDS, 4, 128, 256), BF16),
        ),
        in_specs=[smem, smem, vmem, vmem, vmem, vmem, vmem, hbm],
        out_specs=(hbm, hbm),
        scratch_shapes=[
            pltpu.VMEM((2, ROUNDS, SIDE, SIDE, 2, 16, 512), BF16),
            pltpu.VMEM((SIDE, SIDE, 16, 128), BF16),
            pltpu.VMEM((16, 64, 1024), BF16),
            pltpu.VMEM((8, 128, 1152), BF16),
            pltpu.VMEM((2, 512, 256), BF16),
            pltpu.VMEM((128, 256), BF16),
            pltpu.VMEM((128, 512), F32),
            pltpu.VMEM((256, 1024), BF16),
            pltpu.VMEM((256, 128), BF16),
            pltpu.VMEM((512, 128), F32),
            pltpu.VMEM((ROUNDS, WAVES, 2, 16, 128), BF16),
            pltpu.VMEM((ROUNDS, WAVES, 2, 16, 128), BF16),
            pltpu.VMEM((8, 512), F32),
            pltpu.VMEM((512, 128), F32),
            pltpu.VMEM((32, 512), F32),
            pltpu.VMEM((32, 512), F32),
            pltpu.VMEM((64, 512), F32),
            pltpu.VMEM((64, 512), F32),
            pltpu.VMEM((4, HALF, 512), BF16),
            pltpu.VMEM((ROUNDS, 4, 128, 256), BF16),
            dma((2, 3)), dma((2, 3)),
            dma((2, ROUNDS)), dma((2, ROUNDS, 3)),
            dma((2,)), dma((2,)),
            dma((ROUNDS,)), dma((ROUNDS,)),
            dma(()), dma((4,)), dma((ROUNDS,)),
        ],
        compiler_params=pltpu.CompilerParams(
            collective_id=0, has_side_effects=True, vmem_limit_bytes=48 * MIB
        ),
        cost_estimate=pl.CostEstimate(flops=4 << 30, bytes_accessed=12 * MIB, transcendentals=0),
    )(
        wavenumbers, cycle_points, wavenumbers.reshape(1, 256), divergence, analysis, synthesis,
        helmholtz.reshape(1, 128), jnp.swapaxes(legendre, 1, 2),
    )
    return pl.pallas_call(
        grid_kernel,
        out_shape=jax.ShapeDtypeStruct((1, 4, LON, 128), BF16),
        in_specs=[smem, hbm, hbm],
        out_specs=hbm,
        scratch_shapes=[
            pltpu.VMEM((4, HALF, 512), BF16),
            pltpu.VMEM((4, ROUNDS, 128, 256), BF16),
            pltpu.VMEM((LON, 128), F32),
            pltpu.VMEM((4, LON, 128), BF16),
            dma((4, 2)), dma((4,)), dma((4, 2)),
        ],
        compiler_params=pltpu.CompilerParams(vmem_limit_bytes=40 * MIB),
        cost_estimate=pl.CostEstimate(flops=4 << 30, bytes_accessed=13 * MIB, transcendentals=0),
    )(cycle_points, basis, values)


def solution(mesh):
    placed = (P("wave", None, "col", None), P(), P(), P(), P("wave", None, "col"), P(), P())
    return jax.shard_map(
        on_device,
        mesh=mesh,
        in_specs=placed,
        out_specs=P("col", "wave", None, None),
        check_vma=False,
    )
```

time: 81.6 us -> 75.3 us (0.923)
  Pallas kernels: 77 us -> 64.9 us
  local copies, waits for them, and re-layouts: 4.47 us -> 9.89 us
    pallas_call x1 -> x2, Pallas kernels: 77 us -> 64.9 us  [the longest x1 55.9 us: on_device(): pl.pallas_call(gather_kernel, out_shape=(jax.ShapeDtypeStruct((4, HALF, 5...]
    unnamed x1 -> x18, local copies, waits for them, and re-layouts: 4.47 us -> 9.89 us
where the time goes in v2:
time: 75.3 us; the launch traced here: 74.9 us
  Pallas kernels  64.9 us (86%)
  local copies, waits for them, and re-layouts  9.89 us (13%)
    pallas_call x1, Pallas kernels, on_device(): pl.pallas_call(gather_kernel, out_shape=(jax.ShapeDtypeStruct((4, HALF, 5...  55.9 us
    unnamed x18, local copies, waits for them, and re-layouts  9.89 us
    pallas_call x1, Pallas kernels, on_device(): pl.pallas_call(grid_kernel, out_shape=jax.ShapeDtypeStruct((1, 4, LON, 12...  8.93 us

profile of v2, /device:TPU:1, one launch (start us, length us, event | category | flops | bytes accessed | tf_op | source)
XLA Modules:
  0.0 74.9 jit_solution(4669398281747676971)
XLA Ops:
  0.0 0.0 copy-start
  0.0 1.6 %copy-done = bf16[16,1024,64]{1,2,0:T(8,128)(2,1)S(1)} copy-done((bf16[16,1024,64]{1,2,0:T(8,128)(2,1)S(1)}, bf16[16,1024,64]{1,2,0:T(8,128)(2,1)}, u32[]{:S(2)}) %copy-start) | copy-done | bytes 2097176
  1.6 0.0 copy-start.1
  1.6 1.2 %copy-done.1 = f32[16,2,8,1024]{3,2,1,0:T(8,128)S(1)} copy-done((f32[16,2,8,1024]{3,2,1,0:T(8,128)S(1)}, f32[16,2,8,1024]{3,2,1,0:T(8,128)}, u32[]{:S(2)}) %copy-start.1) | copy-done | bytes 1048600
  2.8 0.0 copy-start.2
  2.8 0.8 %copy-done.2 = f32[128,128]{1,0:T(8,128)S(1)} copy-done((f32[128,128]{1,0:T(8,128)S(1)}, f32[128,128]{1,0:T(8,128)}, u32[]{:S(2)}) %copy-start.2) | copy-done | bytes 65560
  3.7 0.0 copy-start.3
  3.7 0.8 %copy-done.3 = f32[128,128]{1,0:T(8,128)S(1)} copy-done((f32[128,128]{1,0:T(8,128)S(1)}, f32[128,128]{1,0:T(8,128)}, u32[]{:S(2)}) %copy-start.3) | copy-done | bytes 65560
  4.5 0.0 copy-start.4
  4.5 0.7 copy-done.4
  5.2 0.0 copy-start.6
  5.2 0.7 copy-done.6
  5.9 0.0 copy-start.7
  5.9 0.7 copy-done.7
  6.5 0.0 copy-start.5
  6.5 55.9 %shard_map.73 = (bf16[4,2048,512]{2,1,0:T(8,128)(2,1)}, bf16[4,4,128,256]{3,2,1,0:T(8,128)(2,1)S(1)}) custom-call(s32[256]{0:T(256)S(1)} %copy-done.6, s32[1024]{0:T(1024)S(1)} %copy-done.4, s32[1,256]{1,0:T(1,128)S(1)} %bitcast.4, f32[16,2,8,1024]{3,2,1,0:T(8,128)S(1)} %copy-done.1, f32[128,128]{1,0:T(8,128)S(1)} %copy-done.2, f32[128,128]{1,0:T(8,128)S(1)} %copy-done.3, ...), custom_call_target="tpu_custom_call" | custom-call | flops 4294967296 | bytes 12582912 | tf_op jit(solution)/shard_map/pallas_call | solution.py:435
  62.5 0.0 copy-done.5
  62.5 0.0 copy-start.8
  62.5 3.4 %copy-done.8 = bf16[4,2048,512]{2,1,0:T(8,128)(2,1)S(1)} copy-done((bf16[4,2048,512]{2,1,0:T(8,128)(2,1)S(1)}, bf16[4,2048,512]{2,1,0:T(8,128)(2,1)}, u32[]{:S(2)}) %copy-start.8) | copy-done | bytes 8388632
  65.9 8.9 %shard_map.74 = bf16[1,4,4096,128]{3,2,1,0:T(8,128)(2,1)} custom-call(s32[1024]{0:T(1024)S(1)} %copy-done.5, bf16[4,2048,512]{2,1,0:T(8,128)(2,1)S(1)} %copy-done.8, bf16[4,4,128,256]{3,2,1,0:T(8,128)(2,1)S(1)} %get-tuple-element.8.values_hbm), custom_call_target="tpu_custom_call" | custom-call | flops 4294967296 | bytes 13631488 | tf_op jit(solution)/shard_map/pallas_call | solution.py:478
Async XLA Ops:
  0.0 1.6 %copy-start = (bf16[16,1024,64]{1,2,0:T(8,128)(2,1)S(1)}, bf16[16,1024,64]{1,2,0:T(8,128)(2,1)}, u32[]{:S(2)}) copy-start(bf16[16,1024,64]{1,2,0:T(8,128)(2,1)} %param.11) | copy-start | bytes 6291460
  1.6 1.2 %copy-start.1 = (f32[16,2,8,1024]{3,2,1,0:T(8,128)S(1)}, f32[16,2,8,1024]{3,2,1,0:T(8,128)}, u32[]{:S(2)}) copy-start(f32[16,2,8,1024]{3,2,1,0:T(8,128)} %div.1) | copy-start | bytes 3145732
  2.8 0.8 %copy-start.2 = (f32[128,128]{1,0:T(8,128)S(1)}, f32[128,128]{1,0:T(8,128)}, u32[]{:S(2)}) copy-start(f32[128,128]{1,0:T(8,128)} %analysis.1) | copy-start | bytes 196612
  3.7 0.8 %copy-start.3 = (f32[128,128]{1,0:T(8,128)S(1)}, f32[128,128]{1,0:T(8,128)}, u32[]{:S(2)}) copy-start(f32[128,128]{1,0:T(8,128)} %synthesis.1) | copy-start | bytes 196612
  4.5 0.7 copy-start.4
  5.2 0.7 copy-start.6
  5.9 0.7 copy-start.7
  6.5 55.9 %copy-start.5 = (s32[1024]{0:T(1024)S(1)}, s32[1024]{0:T(1024)}, u32[]{:S(2)}) copy-start(s32[1024]{0:T(1024)} %cp_s.3) | copy-start | bytes 12292
  62.5 3.4 %copy-start.8 = (bf16[4,2048,512]{2,1,0:T(8,128)(2,1)S(1)}, bf16[4,2048,512]{2,1,0:T(8,128)(2,1)}, u32[]{:S(2)}) copy-start(bf16[4,2048,512]{2,1,0:T(8,128)(2,1)} %get-tuple-element.7.basis_hbm) | copy-start | bytes 25165828

commit v3 on v2

--- a/solution.py
+++ b/solution.py
@@ -310,7 +310,8 @@
     def z_start(rho):
         G[rho] = G32[...].reshape(WAVES, 2, 16, 128).astype(BF16)
 
-        def one(d, _):
+        def one(k, _):
+            d = 8 + (1 - 2 * lax.rem(k, 2)) * (k // 2)
             to = lax.rem(w + d, WAVES)
             send(G.at[rho, to], F.at[rho, w], (to, col), z_send.at[rho], z_recv.at[rho]).start()
             return 0
@@ -335,25 +336,29 @@
             V[rho, u, :, 128:256] = (part * sign).astype(BF16)
         values_copy(rho).start()
 
-    for rho in range(ROUNDS):
+    def relay(rho):
         for kind in range(2):
             for which in range(2):
                 p2_row(kind, rho, which)
                 p2(kind, rho, 2 + which).start()
         if rho < 2:
             p2_direct(rho + 2)
-        if rho == 0:
-            lax.fori_loop(BEFORE + 1, 4, make_basis, 0)
-            xe_all(1).wait_recv()
-            n = jnp.zeros((1, 128), F32)
-            for i in range(8):
-                lo, _ = low_of(i)
-                n = jnp.where(iota((1, 128), 1) == i, (1023 - lo).astype(F32), n)
-            out = solve(XE[...].reshape(256, 128), 0, n, 128)
-            for r in range(2):
-                CE[r * 128:(r + 1) * 128] = out[r]
-        if rho >= 2:
-            make_values(rho - 2)
+
+    relay(0)
+    lax.fori_loop(BEFORE + 1, 4, make_basis, 0)
+    xe_all(1).wait_recv()
+    n = jnp.zeros((1, 128), F32)
+    for i in range(8):
+        lo, _ = low_of(i)
+        n = jnp.where(iota((1, 128), 1) == i, (1023 - lo).astype(F32), n)
+    out = solve(XE[...].reshape(256, 128), 0, n, 128)
+    for r in range(2):
+        CE[r * 128:(r + 1) * 128] = out[r]
+    for rho in range(ROUNDS):
+        if rho < 3:
+            relay(rho + 1)
+        if rho == 3:
+            make_values(0)
         for kind in range(2):
             p2_relayed(kind, rho)
             field(kind, rho)
@@ -369,14 +374,14 @@
         xe_all(stage).wait_send()
     for u in range(4):
         basis_copy(u).wait()
-    make_values(2)
-    make_values(3)
+    for rho in range(1, ROUNDS):
+        make_values(rho)
     for rho in range(ROUNDS):
         z_all(rho).wait_send()
         values_copy(rho).wait()
 
 
-def grid_kernel(cp_s, basis_hbm, values_hbm, out_hbm, basis, V, D, stage, basis_sem, values_sem, out_sem):
+def grid_kernel(cp_s, basis_hbm, values_hbm, out_hbm, basis, V, D, PL, stage, basis_sem, values_sem, out_sem):
     first = lax.axis_index("col") * 64 + lax.axis_index("wave") * 4
 
     def basis_copy(u, b):
@@ -387,43 +392,59 @@
         return pltpu.make_async_copy(values_hbm.at[:, u], V.at[u], values_sem.at[u])
 
     def out_copy(u, b):
-        at = pl.ds(b * HALF, HALF)
+        at = pl.ds(b * 1024, 1024)
         return pltpu.make_async_copy(stage.at[u, at], out_hbm.at[0, u, at], out_sem.at[u, b])
 
-    for u in range(4):
+    def fetch(u):
         values_copy(u).start()
         for b in range(2):
             basis_copy(u, b).start()
-    for u in range(4):
+
+    def sums(u):
+        values = V[u].reshape(512, 256)
+        k = u % 2
+        for b in range(2):
+            both = dot(basis[u, b * 1024:(b + 1) * 1024], values)
+            D[k, 1024 + b * 1024:2048 + b * 1024] = both[:, 128:256]
+            if b == 0:
+                stage[u, 0:1024] = both[:, 0:128].astype(BF16)
+            else:
+                PL[k, 1024:2048] = both[:, 0:128]
+
+    def place(u):
         points = cp_s[first + u]
         half = points >> 1
-        values_copy(u).wait()
-        values = V[u].reshape(512, 256)
-
+        k = u % 2
         def turned(at):
-            return D[pl.ds(pl.multiple_of(1024 + at - half, 8), 512)]
-
-        for b in range(2):
-            basis_copy(u, b).wait()
-            both = dot(basis[u, b * 1024:(b + 1) * 1024], values)
-            D[1024 + b * 1024:2048 + b * 1024] = both[:, 128:256]
-            plus = both[:, 0:128]
-            if b == 0:
-                stage[u, 0:1024] = plus.astype(BF16)
+            return D[k, pl.ds(pl.multiple_of(1024 + at - half, 8), 256)]
+        for q in range(4, 16):
+            at = q * 256
+            j = iota((256, 128), 0) + at
+            if q < 8:
+                value = jnp.where(j < half, PL[k, at:at + 256], turned(at))
             else:
-                for k in range(2):
-                    at = 1024 + k * 512
-                    j = iota((512, 128), 0) + at
-                    here = plus[k * 512:(k + 1) * 512]
-                    stage[u, at:at + 512] = jnp.where(j < half, here, turned(at)).astype(BF16)
-        out_copy(u, 0).start()
-        for k in range(4):
-            at = HALF + k * 512
-            j = iota((512, 128), 0) + at
-            stage[u, at:at + 512] = jnp.where(j < points, turned(at), 0.0).astype(BF16)
-        out_copy(u, 1).start()
+                value = jnp.where(j < points, turned(at), 0.0)
+            stage[u, at:at + 256] = value.astype(BF16)
+
+    for u in range(2):
+        fetch(u)
+    for u in range(5):
+        if u < 4:
+            values_copy(u).wait()
+            basis_copy(u, 0).wait()
+            basis_copy(u, 1).wait()
+            if u < 2:
+                fetch(u + 2)
+            sums(u)
+        if u > 0:
+            place(u - 1)
+        if u < 4:
+            out_copy(u, 0).start()
+        if u > 0:
+            for b in range(1, 4):
+                out_copy(u - 1, b).start()
     for u in range(4):
-        for b in range(2):
+        for b in range(4):
             out_copy(u, b).wait()
 
 
@@ -468,7 +489,7 @@
             dma(()), dma((4,)), dma((ROUNDS,)),
         ],
         compiler_params=pltpu.CompilerParams(
-            collective_id=0, has_side_effects=True, vmem_limit_bytes=48 * MIB
+            collective_id=0, has_side_effects=True, vmem_limit_bytes=60 * MIB
         ),
         cost_estimate=pl.CostEstimate(flops=4 << 30, bytes_accessed=12 * MIB, transcendentals=0),
     )(
@@ -483,11 +504,12 @@
         scratch_shapes=[
             pltpu.VMEM((4, HALF, 512), BF16),
             pltpu.VMEM((4, ROUNDS, 128, 256), BF16),
-            pltpu.VMEM((LON, 128), F32),
+            pltpu.VMEM((2, LON, 128), F32),
+            pltpu.VMEM((2, HALF, 128), F32),
             pltpu.VMEM((4, LON, 128), BF16),
-            dma((4, 2)), dma((4,)), dma((4, 2)),
+            dma((4, 2)), dma((4,)), dma((4, 4)),
         ],
-        compiler_params=pltpu.CompilerParams(vmem_limit_bytes=40 * MIB),
+        compiler_params=pltpu.CompilerParams(vmem_limit_bytes=60 * MIB),
         cost_estimate=pl.CostEstimate(flops=4 << 30, bytes_accessed=13 * MIB, transcendentals=0),
     )(cycle_points, basis, values)
 

time: 75.3 us -> 54.8 us (0.73)
  Pallas kernels: 64.9 us -> 54.5 us
  local copies, waits for them, and re-layouts: 9.89 us -> 0 us
    unnamed x18 -> x0, local copies, waits for them, and re-layouts: 9.89 us -> none
    pallas_call x1, Pallas kernels: 55.9 us -> 47.1 us  [on_device(): pl.pallas_call(gather_kernel, out_shape=(jax.ShapeDtypeStruct((4, HALF, 5...]
    pallas_call x1, Pallas kernels: 8.93 us -> 7.41 us  [on_device(): pl.pallas_call(grid_kernel, out_shape=jax.ShapeDtypeStruct((1, 4, LON, 12...]
where the time goes in v3:
time: 54.8 us; the launch traced here: 54.7 us
  Pallas kernels  54.5 us (99%)
    pallas_call x1, Pallas kernels, on_device(): pl.pallas_call(gather_kernel, out_shape=(jax.ShapeDtypeStruct((4, HALF, 5...  47.1 us
    pallas_call x1, Pallas kernels, on_device(): pl.pallas_call(grid_kernel, out_shape=jax.ShapeDtypeStruct((1, 4, LON, 12...  7.41 us

profile of v3, /device:TPU:1, one launch (start us, length us, event | category | flops | bytes accessed | tf_op | source)
XLA Modules:
  0.0 54.7 jit_solution(2683992600097499638)
XLA Ops:
  0.0 47.1 %shard_map.73 = (bf16[4,2048,512]{2,1,0:T(8,128)(2,1)}, bf16[4,4,128,256]{3,2,1,0:T(8,128)(2,1)}) custom-call(s32[256]{0:T(256)} %wn_s.1, s32[1024]{0:T(1024)} %cp_s.3, s32[1,256]{1,0:T(1,128)} %bitcast.4, f32[16,2,8,1024]{3,2,1,0:T(8,128)} %div.1, f32[128,128]{1,0:T(8,128)} %analysis.1, f32[128,128]{1,0:T(8,128)} %synthesis.1, f32[1,128]{1,0:T(1,128)} %bitcast.5, ...), custom_call_target="tpu_custom_call" | custom-call | flops 4294967296 | bytes 12582912 | tf_op jit(solution)/shard_map/pallas_call | solution.py:456
  47.1 7.4 %shard_map.74 = bf16[1,4,4096,128]{3,2,1,0:T(8,128)(2,1)} custom-call(s32[1024]{0:T(1024)} %cp_s.3, bf16[4,2048,512]{2,1,0:T(8,128)(2,1)} %get-tuple-element.7.basis_hbm, bf16[4,4,128,256]{3,2,1,0:T(8,128)(2,1)} %get-tuple-element.8.values_hbm), custom_call_target="tpu_custom_call" | custom-call | flops 4294967296 | bytes 13631488 | tf_op jit(solution)/shard_map/pallas_call | solution.py:499

commit v4 on v3

v4 whole, which is shorter than its diff:
```python
import math

import jax
import jax.numpy as jnp
from jax import lax
from jax.experimental import pallas as pl
from jax.experimental.pallas import tpu as pltpu
from jax.sharding import PartitionSpec as P

MESH = pl.DeviceIdType.MESH
F32 = jnp.float32
BF16 = jnp.bfloat16
LON = 4096
WAVES = 16
HALF = LON // 2
SIDE = 4
ROUNDS = 2
PAIRS = 8
BEFORE = 2
MIB = 1 << 20


def iota(shape, dim):
    return lax.broadcasted_iota(jnp.int32, shape, dim)


def dot(a, b):
    return jnp.dot(a, b, preferred_element_type=F32)


def cos_sin(turn):
    quadrant = jnp.floor(turn + 0.5)
    x = (turn - quadrant) * (0.5 * math.pi)
    z = x * x
    s = x * (1.0 + z * (-1.0 / 6 + z * (1.0 / 120 + z * (-1.0 / 5040 + z * (1.0 / 362880)))))
    c = 1.0 + z * (-0.5 + z * (1.0 / 24 + z * (-1.0 / 720 + z * (1.0 / 40320))))
    odd = (quadrant == 1.0) | (quadrant == 3.0)
    cosine = jnp.where(odd, s, c)
    sine = jnp.where(odd, c, s)
    cosine = jnp.where((quadrant == 1.0) | (quadrant == 2.0), -cosine, cosine)
    sine = jnp.where((quadrant == 2.0) | (quadrant == 3.0), -sine, sine)
    return cosine, sine


def gather_kernel(
    wn_s, cp_s, wn_v, div, analysis, synthesis, helm, leg_hbm, basis, V,
    X, N, XE, leg, OL, LN, RL, LP, AHL, SS, HM, C, CE, G32, G, F, ML, SG, UA, VA, CB, SB,
    p1_send, p1_recv, p2_send, p2_recv, xe_send, xe_recv, ln_send, ln_recv, z_send, z_recv,
    leg_sem,
):
    w = lax.axis_index("wave")
    col = lax.axis_index("col")
    cx, cy = col // SIDE, col % SIDE

    def wrap(v, n=SIDE):
        return lax.rem(v + n, n)

    first = (cx, cy)
    second = (cy, cx)

    def toward(d):
        by = 1 - 2 * (d % 2)
        return by, -by

    def held(kind, rho):
        return kind * 4 + 2 * rho + ((first[kind] + 1) // 2) % 2

    def given(kind, rho):
        return kind * 4 + 2 * rho + 1 - ((first[kind] + 1) // 2) % 2

    def column(kind, d1, d2):
        return d1 * SIDE + d2 if kind == 0 else d2 * SIDE + d1

    def step_first(kind, by):
        return (w, column(kind, wrap(first[kind] + by), second[kind]))

    def step_second(kind, by):
        return (w, column(kind, first[kind], wrap(second[kind] + by)))

    barrier = pltpu.get_barrier_semaphore()
    for kind in range(2):
        for by in (1, 2, 3):
            pl.semaphore_signal(barrier, inc=1, device_id=step_first(kind, by), device_id_type=MESH)

    partner_col = [step_first(kind, toward(first[kind])[0])[1] for kind in range(2)]

    def greet(d, _):
        for to in (col, partner_col[0], partner_col[1]):
            pl.semaphore_signal(
                barrier, inc=1, device_id=(lax.rem(w + d, WAVES), to), device_id_type=MESH
            )
        return 0

    lax.fori_loop(1, WAVES, greet, 0)
    leg_copy = pltpu.make_async_copy(leg_hbm, leg, leg_sem)
    leg_copy.start()

    def low_of(i):
        m = wn_s[w * 16 + 2 * i]
        return jnp.minimum(m, 1023 - m), jnp.where(m > 511, 1, 0)

    lanes = iota((16, 512), 1)
    tile_lane = iota((16, 128), 1)
    extra = jnp.zeros((16, 128), F32)
    for kind in range(2):
        for rho in range(ROUNDS):
            for keep in range(2):
                i = held(kind, rho) if keep else given(kind, rho)
                lo, swap = low_of(i)
                low = div[2 * i + swap].reshape(16, 1024)
                high = div[2 * i + 1 - swap].reshape(16, 1024)
                rolled = pltpu.roll(high[:, 512:], lo, 1)
                own = X.at[kind, rho, second[kind], first[kind]] if keep else N.at[kind, rho]
                own[0] = jnp.where(lanes >= lo, low[:, :512], rolled).astype(BF16)
                own[1] = low[:, 512:].astype(BF16)
                moved = pltpu.roll(rolled[:, 384:], i + 1, 1)
                extra = jnp.where(tile_lane == i, moved, extra)
    XE[cy, cx] = extra.astype(BF16)

    a_full = analysis[...]
    a_hi = a_full.astype(BF16)
    a_lo = (a_full - a_hi.astype(F32)).astype(BF16)
    row = iota((128, 256), 0)
    j = iota((128, 256), 1)
    j2, j1 = j >> 6, (j >> 4) & 3
    for kind in range(2):
        level = (j1 * SIDE + j2 if kind == 0 else j2 * SIDE + j1) * 8 + (j & 7)
        for r in range(2):
            pick = jnp.where((row == level) & (((j >> 3) & 1) == r), 1.0, 0.0).astype(BF16)
            AHL[kind, r * 128:(r + 1) * 128] = dot(a_hi, pick).astype(BF16)
            AHL[kind, 256 + r * 128:256 + (r + 1) * 128] = dot(a_lo, pick).astype(BF16)
    s_full = synthesis[...]
    s_hi = s_full.astype(BF16)
    SS[:, 0:128] = s_hi
    SS[:, 128:256] = (s_full - s_hi.astype(F32)).astype(BF16)
    h_rows = jnp.broadcast_to(helm[...], (128, 128)).T
    for q in range(4):
        HM[:, q * 128:(q + 1) * 128] = h_rows

    lane = iota((256, 512), 1)
    slot = ((lane >> 2) & 15) * 16 + 2 * (lane >> 6)
    choose = jnp.where(iota((256, 512), 0) == slot, 1.0, 0.0).astype(BF16)
    wn = jnp.broadcast_to(wn_v[...], (16, 256))
    upper = dot((wn >> 5).astype(F32).astype(BF16), choose)
    lower = dot((wn & 31).astype(F32).astype(BF16), choose)
    m0 = (upper * 32.0 + lower)[0:8]
    m_lo = jnp.minimum(m0, 1023.0 - m0)
    m_lane = jnp.where((iota((8, 512), 1) & 1) == 1, 1023.0 - m_lo, m_lo)
    ML[...] = m_lane
    sign = 1.0 - 2.0 * (m_lane - 2.0 * jnp.floor(m_lane * 0.5))
    for q in range(4):
        part = jnp.broadcast_to(sign[0:1, q * 128:(q + 1) * 128], (128, 128))
        SG[q * 128:(q + 1) * 128] = part.T

    def make_angles(u):
        latitude = col * 64 + w * 4 + u

        def angle(index, count):
            points = jnp.full((count, 512), cp_s[latitude], jnp.int32).astype(F32)
            inverse = 1.0 / points
            product = index.astype(F32) * jnp.broadcast_to(ML[0:1], (count, 512))
            rest = product - jnp.floor(product * inverse) * points
            rest = jnp.where(rest < 0.0, rest + points, rest)
            rest = jnp.where(rest >= points, rest - points, rest)
            return cos_sin(rest * (4.0 * inverse))

        c, s = angle(iota((32, 512), 0) * 64, 32)
        weight = jnp.where(ML[0:1] == 0.0, 1.0, 2.0) / math.sqrt(256.0)
        imaginary = ((iota((32, 512), 1) >> 1) & 1) == 1
        c, s = weight * c, -weight * s
        UA[...] = jnp.where(imaginary, s, c)
        VA[...] = jnp.where(imaginary, -c, s)
        c, s = angle(iota((64, 512), 0), 64)
        CB[...] = c
        SB[...] = s

    def make_basis(u, _):
        make_angles(u)

        def rows(a8, _):
            some = pl.ds(pl.multiple_of(a8 * 8, 8), 8)
            for q in range(4):
                at = pl.ds(q * 128, 128)
                ua, va, cb, sb = UA[some, at], VA[some, at], CB[:, at], SB[:, at]
                for k in range(8):
                    value = ua[k:k + 1] * cb + va[k:k + 1] * sb
                    start = pl.multiple_of(a8 * 512, 512) + k * 64
                    basis[u, pl.ds(start, 64), at] = value.astype(BF16)
            return 0

        lax.fori_loop(0, HALF // 512, rows, 0)
        return 0

    def leg_pack(i, to):
        lo, swap = low_of(i)
        low = leg.at[2 * i + swap]
        high = leg.at[2 * i + 1 - swap]
        rolled = pltpu.roll(high[:, 512:].astype(F32), lo, 1)
        both = jnp.where(iota((64, 512), 1) >= lo, low[:, 0:512].astype(F32), rolled)
        to[:, 0:512] = both.astype(BF16)
        to[:, 512:1024] = low[:, 512:]
        moved = pltpu.roll(rolled[:, 384:], i + 1, 1)
        to[:, 1024:1152] = jnp.where(iota((64, 128), 1) == i, moved, 0.0).astype(BF16)

    def leg_spread(kind, rho, at, block):
        lo, _ = low_of(held(kind, rho))
        p = iota((64, 512), 1)
        both = block[:, 0:512].astype(F32)
        to = LP.at[kind, rho]
        to[at:at + 64, 0:512] = jnp.where(p >= lo, both, 0.0).astype(BF16)
        to[at + 64:at + 128, 0:512] = jnp.where(p < lo, both, 0.0).astype(BF16)
        to[at:at + 64, 512:1024] = block[:, 512:1024]
        to[at + 64:at + 128, 512:1024] = jnp.zeros((64, 512), BF16)
        to[at:at + 64, 1024:1152] = jnp.zeros((64, 128), BF16)
        to[at + 64:at + 128, 1024:1152] = block[:, 1024:1152]

    leg_copy.wait()
    for rho in range(ROUNDS):
        for kind in range(2):
            leg_pack(given(kind, rho), LN.at[kind, rho])
    lax.fori_loop(0, BEFORE, make_basis, 0)
    pl.semaphore_wait(barrier, 6 + 3 * (WAVES - 1))

    def send(src, dst, to, send_sem, recv_sem):
        return pltpu.make_async_remote_copy(
            src_ref=src, dst_ref=dst, send_sem=send_sem, recv_sem=recv_sem,
            device_id=to, device_id_type=MESH,
        )

    def bytes_of(ref, send_sem, recv_sem):
        return send(ref, ref, step_first(0, 1), send_sem, recv_sem)

    def p1_start(kind, rho):
        to = X.at[kind, rho, second[kind], first[kind]]
        partner, other = toward(first[kind])
        for src, by in ((N.at[kind, rho], 2), (N.at[kind, rho], partner), (to, other)):
            send(src, to, step_first(kind, by), p1_send.at[kind, rho], p1_recv.at[kind, rho]).start()

    def p1_all(kind, rho):
        ref = X.at[kind, rho, second[kind], pl.ds(0, 3)]
        return bytes_of(ref, p1_send.at[kind, rho], p1_recv.at[kind, rho])

    def p2(kind, rho, which):
        d2 = second[kind]
        partner, other = toward(d2)
        ref = X.at[kind, rho, wrap(d2 + partner) if which == 2 else d2]
        to = step_second(kind, partner if which == 0 else other)
        return send(ref, ref, to, p2_send.at[kind, rho], p2_recv.at[kind, rho, which])

    def p2_direct(rho):
        for which in range(2):
            for kind in range(2):
                p2(kind, rho, which).start()

    def p2_arrived(kind, rho, which):
        partner, other = toward(second[kind])
        ref = X.at[kind, rho, wrap(second[kind] + (partner, other, 2)[which])]
        bytes_of(ref, p2_send.at[kind, rho], p2_recv.at[kind, rho, which]).wait_recv()

    def ln(kind, rho):
        to = step_first(kind, toward(first[kind])[0])
        return send(LN.at[kind, rho], RL.at[kind, rho], to, ln_send.at[kind, rho], ln_recv.at[kind, rho])

    def xe_start(stage):
        ref = XE.at[cy, cx] if stage == 0 else XE.at[cy]
        for by in (2, 1, 3):
            to = step_first(0, by) if stage == 0 else step_second(0, by)
            send(ref, ref, to, xe_send.at[stage], xe_recv.at[stage]).start()

    def xe_all(stage):
        ref = XE.at[cy, pl.ds(0, 3)] if stage == 0 else XE.at[pl.ds(0, 3)]
        return bytes_of(ref, xe_send.at[stage], xe_recv.at[stage])

    for rho in range(ROUNDS):
        for kind in range(2):
            p1_start(kind, rho)
        if rho == 0:
            xe_start(0)
    for kind in range(2):
        ln(kind, 0).start()

    for rho in range(ROUNDS):
        for kind in range(2):
            leg_pack(held(kind, rho), OL.at[kind, rho])
            leg_spread(kind, rho, 0, OL.at[kind, rho])
    lax.fori_loop(BEFORE, BEFORE + 1, make_basis, 0)
    for rho in range(ROUNDS):
        for kind in range(2):
            p1_all(kind, rho).wait_recv()
        p2_direct(rho)
    for kind in range(2):
        ln(kind, 1).start()
    xe_all(0).wait_recv()
    xe_start(1)
    lax.fori_loop(BEFORE + 1, 4, make_basis, 0)

    def solve(x, kind, n, count):
        modes = dot(AHL[kind], x)
        modes = modes[0:256] + modes[256:512]
        factor = 1.0 / (1.0 + HM[:, 0:count] * (n * (n + 1.0)))
        out = []
        for r in range(2):
            part = modes[r * 128:(r + 1) * 128] * factor
            hi = part.astype(BF16)
            lo = (part - hi.astype(F32)).astype(BF16)
            both = jnp.concatenate([hi, hi], axis=0)
            out.append((dot(SS[...], both) + dot(SS[:, 0:128], lo)).astype(BF16))
        return out

    def field(kind, rho):
        lo, _ = low_of(held(kind, rho))
        for h in range(2):
            p = iota((1, 512), 1) + h * 512
            n = jnp.where(p >= lo, p, p + 1024 - lo).astype(F32)
            x = X[kind, rho, :, :, h].reshape(256, 512)
            out = solve(x, kind, n, 512)
            for r in range(2):
                C[r * 128:(r + 1) * 128, h * 512:(h + 1) * 512] = out[r]
        table = LP.at[kind, rho]
        contract = (((1,), (1,)), ((), ()))
        total = lax.dot_general(table[:, 0:1024], C[...], contract, preferred_element_type=F32)
        total += lax.dot_general(table[:, 1024:1152], CE[...], contract, preferred_element_type=F32)
        for block in range(2):
            for side in range(2):
                for r in range(2):
                    at = block * 128 + side * 64
                    G32[block, pl.ds(r * 2 + side, 64, stride=4)] = (
                        total[at:at + 64, r * 128:(r + 1) * 128]
                    )

    def z_start(kind, rho):
        i = held(kind, rho)
        for block in range(2):
            G[kind, rho, block] = G32[block].reshape(WAVES, 16, 128).astype(BF16)

        def block_to(block, to):
            there = (to, partner_col[kind] if block else col)
            send(G.at[kind, rho, block, to], F.at[i, w], there, z_send.at[kind, rho, block],
                 z_recv.at[i]).start()

        def one(k, _):
            d = 8 + (1 - 2 * lax.rem(k, 2)) * (k // 2)
            to = lax.rem(w + d, WAVES)
            block_to(1, to)
            block_to(0, to)
            return 0

        lax.fori_loop(1, WAVES, one, 0)
        block_to(1, w)
        F[i, w] = G[kind, rho, 0, w]

    def z_sent(kind, rho):
        for block in range(2):
            ref = F.at[0, pl.ds(0, WAVES - 1 + block)]
            bytes_of(ref, z_send.at[kind, rho, block], z_recv.at[0]).wait_send()

    def make_values(kind, rho, mine):
        i = held(kind, rho) if mine else given(kind, rho)
        ref = F.at[i, pl.ds(0, WAVES - 1 if mine else WAVES)]
        bytes_of(ref, z_send.at[kind, rho, 0], z_recv.at[i]).wait_recv()
        sign = SG[pl.ds(pl.multiple_of(i * 64, 64), 64)]
        tiles = F[i].astype(F32).reshape(8, 2, 2, 8, 128)
        top = iota((64, 128), 0) % 8 < 4
        for u2 in range(2):
            even = tiles[:, 0, u2].reshape(64, 128)
            odd = tiles[:, 1, u2].reshape(64, 128)
            swap_even = pltpu.roll(tiles[:, 0, u2], 4, 1).reshape(64, 128)
            swap_odd = pltpu.roll(tiles[:, 1, u2], 4, 1).reshape(64, 128)
            for u1 in range(2):
                part = jnp.where(top, even, swap_odd) if u1 == 0 else jnp.where(top, swap_even, odd)
                V[i, 2 * u2 + u1, :, 0:128] = part.astype(BF16)
                V[i, 2 * u2 + u1, :, 128:256] = (part * sign).astype(BF16)

    def relay(rho):
        for kind in range(2):
            p2_arrived(kind, rho, 0)
            p2(kind, rho, 2).start()

    relay(0)
    xe_all(1).wait_recv()
    n = jnp.zeros((1, 128), F32)
    for i in range(8):
        lo, _ = low_of(i)
        n = jnp.where(iota((1, 128), 1) == i, (1023 - lo).astype(F32), n)
    out = solve(XE[...].reshape(256, 128), 0, n, 128)
    for r in range(2):
        CE[r * 128:(r + 1) * 128] = out[r]
    relay(1)
    for rho in range(ROUNDS):
        for kind in range(2):
            p2_arrived(kind, rho, 1)
            ln(kind, rho).wait_recv()
            leg_spread(kind, rho, 128, RL.at[kind, rho])
            p2_arrived(kind, rho, 2)
            field(kind, rho)
            z_start(kind, rho)

    for kind in range(2):
        for rho in range(ROUNDS):
            make_values(kind, rho, True)
            make_values(kind, rho, False)
            if rho == 0 and kind == 0:
                for k in range(2):
                    for r in range(ROUNDS):
                        p1_all(k, r).wait_send()
                        ln(k, r).wait_send()
                        ref = X.at[k, r, pl.ds(0, 3)]
                        bytes_of(ref, p2_send.at[k, r], p2_recv.at[k, r, 0]).wait_send()
                for stage in range(2):
                    xe_all(stage).wait_send()
    for kind in range(2):
        for rho in range(ROUNDS):
            z_sent(kind, rho)


def grid_kernel(cp_s, basis, V, out_hbm, D, PL, stage, out_sem):
    first = lax.axis_index("col") * 64 + lax.axis_index("wave") * 4

    def out_copy(u, b):
        at = pl.ds(b * 1024, 1024)
        return pltpu.make_async_copy(stage.at[u, at], out_hbm.at[0, u, at], out_sem.at[u, b])

    def sums(u):
        values = V[:, u].reshape(512, 256)
        k = u % 2
        for b in range(2):
            both = dot(basis[u, b * 1024:(b + 1) * 1024], values)
            D[k, 1024 + b * 1024:2048 + b * 1024] = both[:, 128:256]
            if b == 0:
                stage[u, 0:1024] = both[:, 0:128].astype(BF16)
            else:
                PL[k, 1024:2048] = both[:, 0:128]

    def place(u):
        points = cp_s[first + u]
        half = points >> 1
        k = u % 2
        def turned(at):
            return D[k, pl.ds(pl.multiple_of(1024 + at - half, 8), 256)]
        for q in range(4, 16):
            at = q * 256
            j = iota((256, 128), 0) + at
            if q < 8:
                value = jnp.where(j < half, PL[k, at:at + 256], turned(at))
            else:
                value = jnp.where(j < points, turned(at), 0.0)
            stage[u, at:at + 256] = value.astype(BF16)

    for u in range(5):
        if u < 4:
            sums(u)
        if u > 0:
            place(u - 1)
        if u < 4:
            out_copy(u, 0).start()
        if u > 0:
            for b in range(1, 4):
                out_copy(u - 1, b).start()
    for u in range(4):
        for b in range(4):
            out_copy(u, b).wait()


def on_device(divergence, analysis, synthesis, helmholtz, legendre, wavenumbers, cycle_points):
    vmem = pl.BlockSpec(memory_space=pltpu.VMEM)
    smem = pl.BlockSpec(memory_space=pltpu.SMEM)
    hbm = pl.BlockSpec(memory_space=pl.ANY)
    dma = pltpu.SemaphoreType.DMA
    basis, values = pl.pallas_call(
        gather_kernel,
        out_shape=(
            pltpu.VMEM((4, HALF, 512), BF16),
            pltpu.VMEM((PAIRS, 4, 64, 256), BF16),
        ),
        in_specs=[smem, smem, vmem, vmem, vmem, vmem, vmem, hbm],
        out_specs=(vmem, vmem),
        scratch_shapes=[
            pltpu.VMEM((2, ROUNDS, SIDE, SIDE, 2, 16, 512), BF16),
            pltpu.VMEM((2, ROUNDS, 2, 16, 512), BF16),
            pltpu.VMEM((SIDE, SIDE, 16, 128), BF16),
            pltpu.VMEM((16, 64, 1024), BF16),
            pltpu.VMEM((2, ROUNDS, 64, 1152), BF16),
            pltpu.VMEM((2, ROUNDS, 64, 1152), BF16),
            pltpu.VMEM((2, ROUNDS, 64, 1152), BF16),
            pltpu.VMEM((2, ROUNDS, 256, 1152), BF16),
            pltpu.VMEM((2, 512, 256), BF16),
            pltpu.VMEM((128, 256), BF16),
            pltpu.VMEM((128, 512), F32),
            pltpu.VMEM((256, 1024), BF16),
            pltpu.VMEM((256, 128), BF16),
            pltpu.VMEM((2, 256, 128), F32),
            pltpu.VMEM((2, ROUNDS, 2, WAVES, 16, 128), BF16),
            pltpu.VMEM((PAIRS, WAVES, 16, 128), BF16),
            pltpu.VMEM((8, 512), F32),
            pltpu.VMEM((512, 128), F32),
            pltpu.VMEM((32, 512), F32),
            pltpu.VMEM((32, 512), F32),
            pltpu.VMEM((64, 512), F32),
            pltpu.VMEM((64, 512), F32),
            dma((2, ROUNDS)), dma((2, ROUNDS)),
            dma((2, ROUNDS)), dma((2, ROUNDS, 3)),
            dma((2,)), dma((2,)),
            dma((2, ROUNDS)), dma((2, ROUNDS)),
            dma((2, ROUNDS, 2)), dma((PAIRS,)),
            dma(()),
        ],
        compiler_params=pltpu.CompilerParams(
            collective_id=0, has_side_effects=True, vmem_limit_bytes=50 * MIB
        ),
        cost_estimate=pl.CostEstimate(flops=4 << 30, bytes_accessed=12 * MIB, transcendentals=0),
    )(
        wavenumbers, cycle_points, wavenumbers.reshape(1, 256), divergence, analysis, synthesis,
        helmholtz.reshape(1, 128), jnp.swapaxes(legendre, 1, 2),
    )
    return pl.pallas_call(
        grid_kernel,
        out_shape=jax.ShapeDtypeStruct((1, 4, LON, 128), BF16),
        in_specs=[smem, vmem, vmem],
        out_specs=hbm,
        scratch_shapes=[
            pltpu.VMEM((2, LON, 128), F32),
            pltpu.VMEM((2, HALF, 128), F32),
            pltpu.VMEM((4, LON, 128), BF16),
            dma((4, 4)),
        ],
        compiler_params=pltpu.CompilerParams(vmem_limit_bytes=30 * MIB),
        cost_estimate=pl.CostEstimate(flops=4 << 30, bytes_accessed=13 * MIB, transcendentals=0),
    )(cycle_points, basis, values)


def solution(mesh):
    placed = (P("wave", None, "col", None), P(), P(), P(), P("wave", None, "col"), P(), P())
    return jax.shard_map(
        on_device,
        mesh=mesh,
        in_specs=placed,
        out_specs=P("col", "wave", None, None),
        check_vma=False,
    )
```

time: 54.8 us -> 51.7 us (0.943)
  Pallas kernels: 54.5 us -> 51.6 us
    pallas_call x1, Pallas kernels: 7.41 us -> 4.94 us  [on_device(): pl.pallas_call(grid_kernel, out_shape=jax.ShapeDtypeStruct((1, 4, LON, 12...]
where the time goes in v4:
time: 51.7 us; the launch traced here: 51.6 us
  Pallas kernels  51.6 us (100%)
    pallas_call x1, Pallas kernels, on_device(): pl.pallas_call(gather_kernel, out_shape=(pltpu.VMEM((4, HALF, 512), BF16)...  46.6 us
    pallas_call x1, Pallas kernels, on_device(): pl.pallas_call(grid_kernel, out_shape=jax.ShapeDtypeStruct((1, 4, LON, 12...  4.94 us

profile of v4, /device:TPU:1, one launch (start us, length us, event | category | flops | bytes accessed | tf_op | source)
XLA Modules:
  0.0 51.6 jit_solution(14698945900718080630)
XLA Ops:
  0.0 0.0 copy-start
  0.0 46.6 %shard_map.73 = (bf16[4,2048,512]{2,1,0:T(8,128)(2,1)S(1)}, bf16[8,4,64,256]{3,2,1,0:T(8,128)(2,1)S(1)}) custom-call(s32[256]{0:T(256)} %wn_s.1, s32[1024]{0:T(1024)} %cp_s.3, s32[1,256]{1,0:T(1,128)} %bitcast.4, f32[16,2,8,1024]{3,2,1,0:T(8,128)} %div.1, f32[128,128]{1,0:T(8,128)} %analysis.1, f32[128,128]{1,0:T(8,128)} %synthesis.1, f32[1,128]{1,0:T(1,128)} %bitcast.5, ...), custom_call_target="tpu_custom_call" | custom-call | flops 4294967296 | bytes 12582912 | tf_op jit(solution)/shard_map/pallas_call | solution.py:469
  46.7 0.0 copy-done
  46.7 4.9 %shard_map.74 = bf16[1,4,4096,128]{3,2,1,0:T(8,128)(2,1)} custom-call(s32[1024]{0:T(1024)S(1)} %copy-done, bf16[4,2048,512]{2,1,0:T(8,128)(2,1)S(1)} %get-tuple-element.7.basis, bf16[8,4,64,256]{3,2,1,0:T(8,128)(2,1)S(1)} %get-tuple-element.8.V), custom_call_target="tpu_custom_call" | custom-call | flops 4294967296 | bytes 13631488 | tf_op jit(solution)/shard_map/pallas_call | solution.py:515
Async XLA Ops:
  0.0 46.7 %copy-start = (s32[1024]{0:T(1024)S(1)}, s32[1024]{0:T(1024)}, u32[]{:S(2)}) copy-start(s32[1024]{0:T(1024)} %cp_s.3) | copy-start | bytes 12292

commit v5 on v4

--- a/solution.py
+++ b/solution.py
@@ -16,7 +16,7 @@
 SIDE = 4
 ROUNDS = 2
 PAIRS = 8
-BEFORE = 2
+FIRST, SECOND = 1, 2
 MIB = 1 << 20
 
 
@@ -43,10 +43,11 @@
 
 
 def gather_kernel(
-    wn_s, cp_s, wn_v, div, analysis, synthesis, helm, leg_hbm, basis, V,
-    X, N, XE, leg, OL, LN, RL, LP, AHL, SS, HM, C, CE, G32, G, F, ML, SG, UA, VA, CB, SB,
+    wn_hbm, cp_hbm, wn_row, div_hbm, analysis_hbm, synthesis_hbm, helm_hbm, leg_hbm, basis, V,
+    wn_s, cp_s, wn_v, div, analysis, synthesis, helm,
+    X, N, XE, leg, OL, LN, RL, LP, AHL, SS, HM, C, G32, G, F, ML, SG, UA, VA, CB, SB,
     p1_send, p1_recv, p2_send, p2_recv, xe_send, xe_recv, ln_send, ln_recv, z_send, z_recv,
-    leg_sem,
+    leg_sem, in_sem,
 ):
     w = lax.axis_index("wave")
     col = lax.axis_index("col")
@@ -77,6 +78,15 @@
     def step_second(kind, by):
         return (w, column(kind, first[kind], wrap(second[kind] + by)))
 
+    fetches = [
+        pltpu.make_async_copy(src, dst, in_sem.at[k])
+        for k, (src, dst) in enumerate((
+            (wn_hbm, wn_s), (div_hbm, div), (cp_hbm, cp_s), (wn_row, wn_v),
+            (analysis_hbm, analysis), (synthesis_hbm, synthesis), (helm_hbm, helm),
+        ))
+    ]
+    for fetch in fetches:
+        fetch.start()
     barrier = pltpu.get_barrier_semaphore()
     for kind in range(2):
         for by in (1, 2, 3):
@@ -98,6 +108,9 @@
     def low_of(i):
         m = wn_s[w * 16 + 2 * i]
         return jnp.minimum(m, 1023 - m), jnp.where(m > 511, 1, 0)
+
+    for fetch in fetches:
+        fetch.wait()
 
     lanes = iota((16, 512), 1)
     tile_lane = iota((16, 128), 1)
@@ -110,12 +123,143 @@
                 low = div[2 * i + swap].reshape(16, 1024)
                 high = div[2 * i + 1 - swap].reshape(16, 1024)
                 rolled = pltpu.roll(high[:, 512:], lo, 1)
-                own = X.at[kind, rho, second[kind], first[kind]] if keep else N.at[kind, rho]
+                own = X.at[kind, rho, second[kind], 0] if keep else N.at[kind, rho]
                 own[0] = jnp.where(lanes >= lo, low[:, :512], rolled).astype(BF16)
                 own[1] = low[:, 512:].astype(BF16)
                 moved = pltpu.roll(rolled[:, 384:], i + 1, 1)
                 extra = jnp.where(tile_lane == i, moved, extra)
-    XE[cy, cx] = extra.astype(BF16)
+    XE[cy, 0] = extra.astype(BF16)
+
+    def make_angles(u):
+        latitude = col * 64 + w * 4 + u
+
+        def angle(index, count):
+            points = jnp.full((count, 512), cp_s[latitude], jnp.int32).astype(F32)
+            inverse = 1.0 / points
+            product = index.astype(F32) * jnp.broadcast_to(ML[0:1], (count, 512))
+            rest = product - jnp.floor(product * inverse) * points
+            rest = jnp.where(rest < 0.0, rest + points, rest)
+            rest = jnp.where(rest >= points, rest - points, rest)
+            return cos_sin(rest * (4.0 * inverse))
+
+        c, s = angle(iota((32, 512), 0) * 64, 32)
+        weight = jnp.where(ML[0:1] == 0.0, 1.0, 2.0) / math.sqrt(256.0)
+        imaginary = ((iota((32, 512), 1) >> 1) & 1) == 1
+        c, s = weight * c, -weight * s
+        UA[...] = jnp.where(imaginary, s, c)
+        VA[...] = jnp.where(imaginary, -c, s)
+        c, s = angle(iota((64, 512), 0), 64)
+        CB[...] = c
+        SB[...] = s
+
+    def make_basis(u, _):
+        make_angles(u)
+
+        def rows(a8, _):
+            some = pl.ds(pl.multiple_of(a8 * 8, 8), 8)
+            for q in range(4):
+                at = pl.ds(q * 128, 128)
+                ua, va, cb, sb = UA[some, at], VA[some, at], CB[:, at], SB[:, at]
+                for k in range(8):
+                    value = ua[k:k + 1] * cb + va[k:k + 1] * sb
+                    start = pl.multiple_of(a8 * 512, 512) + k * 64
+                    basis[u, pl.ds(start, 64), at] = value.astype(BF16)
+            return 0
+
+        lax.fori_loop(0, HALF // 512, rows, 0)
+        return 0
+
+    def leg_pack(i, to):
+        lo, swap = low_of(i)
+        low = leg.at[2 * i + swap]
+        high = leg.at[2 * i + 1 - swap]
+        rolled = pltpu.roll(high[:, 512:].astype(F32), lo, 1)
+        both = jnp.where(iota((64, 512), 1) >= lo, low[:, 0:512].astype(F32), rolled)
+        to[:, 0:512] = both.astype(BF16)
+        to[:, 512:1024] = low[:, 512:]
+        moved = pltpu.roll(rolled[:, 384:], i + 1, 1)
+        to[:, 1024:1152] = jnp.where(iota((64, 128), 1) == i, moved, 0.0).astype(BF16)
+
+    def leg_spread(kind, rho, at, block):
+        lo, _ = low_of(held(kind, rho))
+        p = iota((64, 512), 1)
+        both = block[:, 0:512].astype(F32)
+        to = LP.at[kind, rho]
+        to[at:at + 64, 0:512] = jnp.where(p >= lo, both, 0.0).astype(BF16)
+        to[at + 64:at + 128, 0:512] = jnp.where(p < lo, both, 0.0).astype(BF16)
+        to[at:at + 64, 512:1024] = block[:, 512:1024]
+        to[at + 64:at + 128, 512:1024] = jnp.zeros((64, 512), BF16)
+        to[at:at + 64, 1024:1152] = jnp.zeros((64, 128), BF16)
+        to[at + 64:at + 128, 1024:1152] = block[:, 1024:1152]
+
+    pl.semaphore_wait(barrier, 6 + 3 * (WAVES - 1))
+
+    def send(src, dst, to, send_sem, recv_sem):
+        return pltpu.make_async_remote_copy(
+            src_ref=src, dst_ref=dst, send_sem=send_sem, recv_sem=recv_sem,
+            device_id=to, device_id_type=MESH,
+        )
+
+    def bytes_of(ref, send_sem, recv_sem):
+        return send(ref, ref, step_first(0, 1), send_sem, recv_sem)
+
+    def p1_start(kind, rho):
+        own = X.at[kind, rho, second[kind], 0]
+        partner, other = toward(first[kind])
+        for src, by in ((N.at[kind, rho], 2), (N.at[kind, rho], partner), (own, other)):
+            to = X.at[kind, rho, second[kind], wrap(-by)]
+            send(src, to, step_first(kind, by), p1_send.at[kind, rho], p1_recv.at[kind, rho]).start()
+
+    def p1_all(kind, rho):
+        ref = X.at[kind, rho, second[kind], pl.ds(0, 3)]
+        return bytes_of(ref, p1_send.at[kind, rho], p1_recv.at[kind, rho])
+
+    def p2(kind, rho, part, which):
+        d2 = second[kind]
+        partner, other = toward(d2)
+        row = wrap(d2 + partner) if which == 2 else d2
+        ref = X.at[kind, rho, row, pl.ds(0, 1) if part == 0 else pl.ds(1, 3)]
+        to = step_second(kind, partner if which == 0 else other)
+        return send(ref, ref, to, p2_send.at[kind, rho], p2_recv.at[kind, rho, part, which])
+
+    def p2_direct(rho, part):
+        for which in range(2):
+            for kind in range(2):
+                p2(kind, rho, part, which).start()
+
+    def p2_arrived(kind, rho, part, which):
+        partner, other = toward(second[kind])
+        row = wrap(second[kind] + (partner, other, 2)[which])
+        ref = X.at[kind, rho, row, pl.ds(0, 1) if part == 0 else pl.ds(1, 3)]
+        bytes_of(ref, p2_send.at[kind, rho], p2_recv.at[kind, rho, part, which]).wait_recv()
+
+    def ln(kind, rho):
+        to = step_first(kind, toward(first[kind])[0])
+        return send(LN.at[kind, rho], RL.at[kind, rho], to, ln_send.at[kind, rho], ln_recv.at[kind, rho])
+
+    def relay(rho, part):
+        for kind in range(2):
+            p2_arrived(kind, rho, part, 0)
+            p2(kind, rho, part, 2).start()
+
+    def xe_start(stage):
+        for by in (2, 1, 3):
+            src = XE.at[cy, 0] if stage == 0 else XE.at[cy]
+            dst = XE.at[cy, 4 - by] if stage == 0 else XE.at[cy]
+            to = step_first(0, by) if stage == 0 else step_second(0, by)
+            send(src, dst, to, xe_send.at[stage], xe_recv.at[stage]).start()
+
+    def xe_all(stage):
+        ref = XE.at[cy, pl.ds(0, 3)] if stage == 0 else XE.at[pl.ds(0, 3)]
+        return bytes_of(ref, xe_send.at[stage], xe_recv.at[stage])
+
+    for rho in range(ROUNDS):
+        for kind in range(2):
+            p1_start(kind, rho)
+        if rho == 0:
+            xe_start(0)
+    for rho in range(ROUNDS):
+        p2_direct(rho, 0)
 
     a_full = analysis[...]
     a_hi = a_full.astype(BF16)
@@ -124,7 +268,8 @@
     j = iota((128, 256), 1)
     j2, j1 = j >> 6, (j >> 4) & 3
     for kind in range(2):
-        level = (j1 * SIDE + j2 if kind == 0 else j2 * SIDE + j1) * 8 + (j & 7)
+        j_first = (j1 + first[kind]) & 3
+        level = column(kind, j_first, j2) * 8 + (j & 7)
         for r in range(2):
             pick = jnp.where((row == level) & (((j >> 3) & 1) == r), 1.0, 0.0).astype(BF16)
             AHL[kind, r * 128:(r + 1) * 128] = dot(a_hi, pick).astype(BF16)
@@ -152,147 +297,26 @@
         part = jnp.broadcast_to(sign[0:1, q * 128:(q + 1) * 128], (128, 128))
         SG[q * 128:(q + 1) * 128] = part.T
 
-    def make_angles(u):
-        latitude = col * 64 + w * 4 + u
-
-        def angle(index, count):
-            points = jnp.full((count, 512), cp_s[latitude], jnp.int32).astype(F32)
-            inverse = 1.0 / points
-            product = index.astype(F32) * jnp.broadcast_to(ML[0:1], (count, 512))
-            rest = product - jnp.floor(product * inverse) * points
-            rest = jnp.where(rest < 0.0, rest + points, rest)
-            rest = jnp.where(rest >= points, rest - points, rest)
-            return cos_sin(rest * (4.0 * inverse))
-
-        c, s = angle(iota((32, 512), 0) * 64, 32)
-        weight = jnp.where(ML[0:1] == 0.0, 1.0, 2.0) / math.sqrt(256.0)
-        imaginary = ((iota((32, 512), 1) >> 1) & 1) == 1
-        c, s = weight * c, -weight * s
-        UA[...] = jnp.where(imaginary, s, c)
-        VA[...] = jnp.where(imaginary, -c, s)
-        c, s = angle(iota((64, 512), 0), 64)
-        CB[...] = c
-        SB[...] = s
-
-    def make_basis(u, _):
-        make_angles(u)
-
-        def rows(a8, _):
-            some = pl.ds(pl.multiple_of(a8 * 8, 8), 8)
-            for q in range(4):
-                at = pl.ds(q * 128, 128)
-                ua, va, cb, sb = UA[some, at], VA[some, at], CB[:, at], SB[:, at]
-                for k in range(8):
-                    value = ua[k:k + 1] * cb + va[k:k + 1] * sb
-                    start = pl.multiple_of(a8 * 512, 512) + k * 64
-                    basis[u, pl.ds(start, 64), at] = value.astype(BF16)
-            return 0
-
-        lax.fori_loop(0, HALF // 512, rows, 0)
-        return 0
-
-    def leg_pack(i, to):
-        lo, swap = low_of(i)
-        low = leg.at[2 * i + swap]
-        high = leg.at[2 * i + 1 - swap]
-        rolled = pltpu.roll(high[:, 512:].astype(F32), lo, 1)
-        both = jnp.where(iota((64, 512), 1) >= lo, low[:, 0:512].astype(F32), rolled)
-        to[:, 0:512] = both.astype(BF16)
-        to[:, 512:1024] = low[:, 512:]
-        moved = pltpu.roll(rolled[:, 384:], i + 1, 1)
-        to[:, 1024:1152] = jnp.where(iota((64, 128), 1) == i, moved, 0.0).astype(BF16)
-
-    def leg_spread(kind, rho, at, block):
-        lo, _ = low_of(held(kind, rho))
-        p = iota((64, 512), 1)
-        both = block[:, 0:512].astype(F32)
-        to = LP.at[kind, rho]
-        to[at:at + 64, 0:512] = jnp.where(p >= lo, both, 0.0).astype(BF16)
-        to[at + 64:at + 128, 0:512] = jnp.where(p < lo, both, 0.0).astype(BF16)
-        to[at:at + 64, 512:1024] = block[:, 512:1024]
-        to[at + 64:at + 128, 512:1024] = jnp.zeros((64, 512), BF16)
-        to[at:at + 64, 1024:1152] = jnp.zeros((64, 128), BF16)
-        to[at + 64:at + 128, 1024:1152] = block[:, 1024:1152]
-
     leg_copy.wait()
     for rho in range(ROUNDS):
         for kind in range(2):
             leg_pack(given(kind, rho), LN.at[kind, rho])
-    lax.fori_loop(0, BEFORE, make_basis, 0)
-    pl.semaphore_wait(barrier, 6 + 3 * (WAVES - 1))
-
-    def send(src, dst, to, send_sem, recv_sem):
-        return pltpu.make_async_remote_copy(
-            src_ref=src, dst_ref=dst, send_sem=send_sem, recv_sem=recv_sem,
-            device_id=to, device_id_type=MESH,
-        )
-
-    def bytes_of(ref, send_sem, recv_sem):
-        return send(ref, ref, step_first(0, 1), send_sem, recv_sem)
-
-    def p1_start(kind, rho):
-        to = X.at[kind, rho, second[kind], first[kind]]
-        partner, other = toward(first[kind])
-        for src, by in ((N.at[kind, rho], 2), (N.at[kind, rho], partner), (to, other)):
-            send(src, to, step_first(kind, by), p1_send.at[kind, rho], p1_recv.at[kind, rho]).start()
-
-    def p1_all(kind, rho):
-        ref = X.at[kind, rho, second[kind], pl.ds(0, 3)]
-        return bytes_of(ref, p1_send.at[kind, rho], p1_recv.at[kind, rho])
-
-    def p2(kind, rho, which):
-        d2 = second[kind]
-        partner, other = toward(d2)
-        ref = X.at[kind, rho, wrap(d2 + partner) if which == 2 else d2]
-        to = step_second(kind, partner if which == 0 else other)
-        return send(ref, ref, to, p2_send.at[kind, rho], p2_recv.at[kind, rho, which])
-
-    def p2_direct(rho):
-        for which in range(2):
-            for kind in range(2):
-                p2(kind, rho, which).start()
-
-    def p2_arrived(kind, rho, which):
-        partner, other = toward(second[kind])
-        ref = X.at[kind, rho, wrap(second[kind] + (partner, other, 2)[which])]
-        bytes_of(ref, p2_send.at[kind, rho], p2_recv.at[kind, rho, which]).wait_recv()
-
-    def ln(kind, rho):
-        to = step_first(kind, toward(first[kind])[0])
-        return send(LN.at[kind, rho], RL.at[kind, rho], to, ln_send.at[kind, rho], ln_recv.at[kind, rho])
-
-    def xe_start(stage):
-        ref = XE.at[cy, cx] if stage == 0 else XE.at[cy]
-        for by in (2, 1, 3):
-            to = step_first(0, by) if stage == 0 else step_second(0, by)
-            send(ref, ref, to, xe_send.at[stage], xe_recv.at[stage]).start()
-
-    def xe_all(stage):
-        ref = XE.at[cy, pl.ds(0, 3)] if stage == 0 else XE.at[pl.ds(0, 3)]
-        return bytes_of(ref, xe_send.at[stage], xe_recv.at[stage])
-
-    for rho in range(ROUNDS):
-        for kind in range(2):
-            p1_start(kind, rho)
+    for rho in range(ROUNDS):
+        for kind in range(2):
+            p1_all(kind, rho).wait_recv()
         if rho == 0:
-            xe_start(0)
+            xe_all(0).wait_recv()
+            xe_start(1)
+        p2_direct(rho, 1)
+    for rho in range(ROUNDS):
+        relay(rho, 0)
     for kind in range(2):
         ln(kind, 0).start()
-
     for rho in range(ROUNDS):
         for kind in range(2):
             leg_pack(held(kind, rho), OL.at[kind, rho])
             leg_spread(kind, rho, 0, OL.at[kind, rho])
-    lax.fori_loop(BEFORE, BEFORE + 1, make_basis, 0)
-    for rho in range(ROUNDS):
-        for kind in range(2):
-            p1_all(kind, rho).wait_recv()
-        p2_direct(rho)
-    for kind in range(2):
-        ln(kind, 1).start()
-    xe_all(0).wait_recv()
-    xe_start(1)
-    lax.fori_loop(BEFORE + 1, 4, make_basis, 0)
+    lax.fori_loop(0, FIRST, make_basis, 0)
 
     def solve(x, kind, n, count):
         modes = dot(AHL[kind], x)
@@ -318,8 +342,7 @@
                 C[r * 128:(r + 1) * 128, h * 512:(h + 1) * 512] = out[r]
         table = LP.at[kind, rho]
         contract = (((1,), (1,)), ((), ()))
-        total = lax.dot_general(table[:, 0:1024], C[...], contract, preferred_element_type=F32)
-        total += lax.dot_general(table[:, 1024:1152], CE[...], contract, preferred_element_type=F32)
+        total = lax.dot_general(table[...], C[...], contract, preferred_element_type=F32)
         for block in range(2):
             for side in range(2):
                 for r in range(2):
@@ -371,12 +394,11 @@
                 V[i, 2 * u2 + u1, :, 0:128] = part.astype(BF16)
                 V[i, 2 * u2 + u1, :, 128:256] = (part * sign).astype(BF16)
 
-    def relay(rho):
-        for kind in range(2):
-            p2_arrived(kind, rho, 0)
-            p2(kind, rho, 2).start()
-
-    relay(0)
+    relay(0, 1)
+    for kind in range(2):
+        ln(kind, 1).start()
+    lax.fori_loop(FIRST, SECOND, make_basis, 0)
+    relay(1, 1)
     xe_all(1).wait_recv()
     n = jnp.zeros((1, 128), F32)
     for i in range(8):
@@ -384,19 +406,21 @@
         n = jnp.where(iota((1, 128), 1) == i, (1023 - lo).astype(F32), n)
     out = solve(XE[...].reshape(256, 128), 0, n, 128)
     for r in range(2):
-        CE[r * 128:(r + 1) * 128] = out[r]
-    relay(1)
-    for rho in range(ROUNDS):
-        for kind in range(2):
-            p2_arrived(kind, rho, 1)
+        C[r * 128:(r + 1) * 128, 1024:1152] = out[r]
+    for rho in range(ROUNDS):
+        for kind in range(2):
+            for part in range(2):
+                p2_arrived(kind, rho, part, 1)
             ln(kind, rho).wait_recv()
             leg_spread(kind, rho, 128, RL.at[kind, rho])
-            p2_arrived(kind, rho, 2)
+            for part in range(2):
+                p2_arrived(kind, rho, part, 2)
             field(kind, rho)
             z_start(kind, rho)
 
-    for kind in range(2):
-        for rho in range(ROUNDS):
+    lax.fori_loop(SECOND, 4, make_basis, 0)
+    for rho in range(ROUNDS):
+        for kind in range(2):
             make_values(kind, rho, True)
             make_values(kind, rho, False)
             if rho == 0 and kind == 0:
@@ -405,7 +429,7 @@
                         p1_all(k, r).wait_send()
                         ln(k, r).wait_send()
                         ref = X.at[k, r, pl.ds(0, 3)]
-                        bytes_of(ref, p2_send.at[k, r], p2_recv.at[k, r, 0]).wait_send()
+                        bytes_of(ref, p2_send.at[k, r], p2_recv.at[k, r, 0, 0]).wait_send()
                 for stage in range(2):
                     xe_all(stage).wait_send()
     for kind in range(2):
@@ -472,9 +496,16 @@
             pltpu.VMEM((4, HALF, 512), BF16),
             pltpu.VMEM((PAIRS, 4, 64, 256), BF16),
         ),
-        in_specs=[smem, smem, vmem, vmem, vmem, vmem, vmem, hbm],
+        in_specs=[hbm] * 8,
         out_specs=(vmem, vmem),
         scratch_shapes=[
+            pltpu.SMEM((256,), jnp.int32),
+            pltpu.SMEM((1024,), jnp.int32),
+            pltpu.VMEM((1, 256), jnp.int32),
+            pltpu.VMEM((16, 2, 8, 1024), F32),
+            pltpu.VMEM((128, 128), F32),
+            pltpu.VMEM((128, 128), F32),
+            pltpu.VMEM((1, 128), F32),
             pltpu.VMEM((2, ROUNDS, SIDE, SIDE, 2, 16, 512), BF16),
             pltpu.VMEM((2, ROUNDS, 2, 16, 512), BF16),
             pltpu.VMEM((SIDE, SIDE, 16, 128), BF16),
@@ -486,8 +517,7 @@
             pltpu.VMEM((2, 512, 256), BF16),
             pltpu.VMEM((128, 256), BF16),
             pltpu.VMEM((128, 512), F32),
-            pltpu.VMEM((256, 1024), BF16),
-            pltpu.VMEM((256, 128), BF16),
+            pltpu.VMEM((256, 1152), BF16),
             pltpu.VMEM((2, 256, 128), F32),
             pltpu.VMEM((2, ROUNDS, 2, WAVES, 16, 128), BF16),
             pltpu.VMEM((PAIRS, WAVES, 16, 128), BF16),
@@ -498,11 +528,11 @@
             pltpu.VMEM((64, 512), F32),
             pltpu.VMEM((64, 512), F32),
             dma((2, ROUNDS)), dma((2, ROUNDS)),
-            dma((2, ROUNDS)), dma((2, ROUNDS, 3)),
+            dma((2, ROUNDS)), dma((2, ROUNDS, 2, 3)),
             dma((2,)), dma((2,)),
             dma((2, ROUNDS)), dma((2, ROUNDS)),
             dma((2, ROUNDS, 2)), dma((PAIRS,)),
-            dma(()),
+            dma(()), dma((7,)),
         ],
         compiler_params=pltpu.CompilerParams(
             collective_id=0, has_side_effects=True, vmem_limit_bytes=50 * MIB

time: 51.7 us -> 46.4 us (0.90)
  Pallas kernels: 51.6 us -> 46.3 us
    pallas_call x1, Pallas kernels: 46.6 us -> 41.3 us  [on_device(): pl.pallas_call(gather_kernel, out_shape=(pltpu.VMEM((4, HALF, 512), BF16)...]
where the time goes in v5:
time: 46.4 us; the launch traced here: 46.3 us
  Pallas kernels  46.3 us (100%)
    pallas_call x1, Pallas kernels, on_device(): pl.pallas_call(gather_kernel, out_shape=(pltpu.VMEM((4, HALF, 512), BF16)...  41.3 us
    pallas_call x1, Pallas kernels, on_device(): pl.pallas_call(grid_kernel, out_shape=jax.ShapeDtypeStruct((1, 4, LON, 12...  5.02 us

profile of v5, /device:TPU:1, one launch (start us, length us, event | category | flops | bytes accessed | tf_op | source)
XLA Modules:
  0.0 46.3 jit_solution(2212769287612374923)
XLA Ops:
  0.0 0.0 copy-start
  0.0 41.3 %shard_map.73 = (bf16[4,2048,512]{2,1,0:T(8,128)(2,1)S(1)}, bf16[8,4,64,256]{3,2,1,0:T(8,128)(2,1)S(1)}) custom-call(s32[256]{0:T(256)} %wn_hbm.1, s32[1024]{0:T(1024)} %cp_s.1, s32[1,256]{1,0:T(1,128)} %bitcast.4, f32[16,2,8,1024]{3,2,1,0:T(8,128)} %div_hbm.1, f32[128,128]{1,0:T(8,128)} %analysis_hbm.1, f32[128,128]{1,0:T(8,128)} %synthesis_hbm.1, ...), custom_call_target="tpu_custom_call" | custom-call | flops 4294967296 | bytes 12582912 | tf_op jit(solution)/shard_map/pallas_call | solution.py:493
  41.3 0.0 copy-done
  41.3 5.0 %shard_map.74 = bf16[1,4,4096,128]{3,2,1,0:T(8,128)(2,1)} custom-call(s32[1024]{0:T(1024)S(1)} %copy-done, bf16[4,2048,512]{2,1,0:T(8,128)(2,1)S(1)} %get-tuple-element.7.basis, bf16[8,4,64,256]{3,2,1,0:T(8,128)(2,1)S(1)} %get-tuple-element.8.V), custom_call_target="tpu_custom_call" | custom-call | flops 4294967296 | bytes 13631488 | tf_op jit(solution)/shard_map/pallas_call | solution.py:545
Async XLA Ops:
  0.0 41.3 %copy-start = (s32[1024]{0:T(1024)S(1)}, s32[1024]{0:T(1024)}, u32[]{:S(2)}) copy-start(s32[1024]{0:T(1024)} %cp_s.1) | copy-start | bytes 12292

commit v6 on v5

--- a/solution.py
+++ b/solution.py
@@ -16,7 +16,7 @@
 SIDE = 4
 ROUNDS = 2
 PAIRS = 8
-FIRST, SECOND = 1, 2
+FIRST, SECOND = 0, 1
 MIB = 1 << 20
 
 
@@ -261,6 +261,24 @@
     for rho in range(ROUNDS):
         p2_direct(rho, 0)
 
+    leg_copy.wait()
+    for rho in range(ROUNDS):
+        for kind in range(2):
+            leg_pack(given(kind, rho), LN.at[kind, rho])
+    for rho in range(ROUNDS):
+        for kind in range(2):
+            p1_all(kind, rho).wait_recv()
+        if rho == 0:
+            xe_all(0).wait_recv()
+            xe_start(1)
+        p2_direct(rho, 1)
+        if rho == 0:
+            for kind in range(2):
+                ln(kind, 0).start()
+    for rho in range(ROUNDS):
+        relay(rho, 0)
+    for kind in range(2):
+        ln(kind, 1).start()
     a_full = analysis[...]
     a_hi = a_full.astype(BF16)
     a_lo = (a_full - a_hi.astype(F32)).astype(BF16)
@@ -297,21 +315,6 @@
         part = jnp.broadcast_to(sign[0:1, q * 128:(q + 1) * 128], (128, 128))
         SG[q * 128:(q + 1) * 128] = part.T
 
-    leg_copy.wait()
-    for rho in range(ROUNDS):
-        for kind in range(2):
-            leg_pack(given(kind, rho), LN.at[kind, rho])
-    for rho in range(ROUNDS):
-        for kind in range(2):
-            p1_all(kind, rho).wait_recv()
-        if rho == 0:
-            xe_all(0).wait_recv()
-            xe_start(1)
-        p2_direct(rho, 1)
-    for rho in range(ROUNDS):
-        relay(rho, 0)
-    for kind in range(2):
-        ln(kind, 0).start()
     for rho in range(ROUNDS):
         for kind in range(2):
             leg_pack(held(kind, rho), OL.at[kind, rho])
@@ -395,8 +398,6 @@
                 V[i, 2 * u2 + u1, :, 128:256] = (part * sign).astype(BF16)
 
     relay(0, 1)
-    for kind in range(2):
-        ln(kind, 1).start()
     lax.fori_loop(FIRST, SECOND, make_basis, 0)
     relay(1, 1)
     xe_all(1).wait_recv()

time: 46.4 us -> 45.9 us (0.989)
  no operation moved by 1% of the time
where the time goes in v6:
time: 45.9 us
  Pallas kernels  45.9 us (100%)
    pallas_call x1, Pallas kernels, on_device(): pl.pallas_call(gather_kernel, out_shape=(pltpu.VMEM((4, HALF, 512), BF16)...  40.9 us
    pallas_call x1, Pallas kernels, on_device(): pl.pallas_call(grid_kernel, out_shape=jax.ShapeDtypeStruct((1, 4, LON, 12...  5.01 us

profile of v6, /device:TPU:1, one launch (start us, length us, event | category | flops | bytes accessed | tf_op | source)
XLA Modules:
  0.0 45.9 jit_solution(16450768599806836202)
XLA Ops:
  0.0 0.0 copy-start
  0.0 40.9 %shard_map.73 = (bf16[4,2048,512]{2,1,0:T(8,128)(2,1)S(1)}, bf16[8,4,64,256]{3,2,1,0:T(8,128)(2,1)S(1)}) custom-call(s32[256]{0:T(256)} %wn_hbm.1, s32[1024]{0:T(1024)} %cp_s.1, s32[1,256]{1,0:T(1,128)} %bitcast.4, f32[16,2,8,1024]{3,2,1,0:T(8,128)} %div_hbm.1, f32[128,128]{1,0:T(8,128)} %analysis_hbm.1, f32[128,128]{1,0:T(8,128)} %synthesis_hbm.1, ...), custom_call_target="tpu_custom_call" | custom-call | flops 4294967296 | bytes 12582912 | tf_op jit(solution)/shard_map/pallas_call | solution.py:494
  40.9 0.0 copy-done
  40.9 5.0 %shard_map.74 = bf16[1,4,4096,128]{3,2,1,0:T(8,128)(2,1)} custom-call(s32[1024]{0:T(1024)S(1)} %copy-done, bf16[4,2048,512]{2,1,0:T(8,128)(2,1)S(1)} %get-tuple-element.7.basis, bf16[8,4,64,256]{3,2,1,0:T(8,128)(2,1)S(1)} %get-tuple-element.8.V), custom_call_target="tpu_custom_call" | custom-call | flops 4294967296 | bytes 13631488 | tf_op jit(solution)/shard_map/pallas_call | solution.py:546
Async XLA Ops:
  0.0 40.9 %copy-start = (s32[1024]{0:T(1024)S(1)}, s32[1024]{0:T(1024)}, u32[]{:S(2)}) copy-start(s32[1024]{0:T(1024)} %cp_s.1) | copy-start | bytes 12292
